TPU v7x, 32 devices: a whole 2x2x4 slice. The times are simulated.
32 devices in a mesh: frame: 16 (over z, x, core), row: 2 (over y).
Axes of the slice: x: 2, y: 2, z: 4, core: 2. Of those that a mesh axis runs over, the one named last changes fastest.
Arguments:
- latents: bfloat16 [64, 32, 32, 320], P('frame', 'row'), may hold values from -20 to 20
- ln_gain: bfloat16 [320], replicated, may hold values from 0.099609375 to 1.8984375
- q_weight: bfloat16 [320, 320], replicated, may hold values from -0.30078125 to 0.30078125
- k_weight: bfloat16 [320, 320], replicated, may hold values from -3 to 3
- v_weight: bfloat16 [320, 320], replicated, may hold values from -0.3125 to 0.3125
- o_weight: bfloat16 [320, 320], replicated, may hold values from -0.3125 to 0.3125
- gn_gain: bfloat16 [320], replicated, may hold values from 0.099609375 to 1.8984375
- conv_weight: bfloat16 [3, 3, 320, 320], replicated, may hold values from -0.109375 to 0.109375
- conv_bias: bfloat16 [320], replicated, may hold values from -3 to 3
Outputs:
- output: bfloat16 [64, 32, 32, 320], P('frame', 'row')
All inputs are finite; a program needn't handle non-finite values.
Results may differ from a plain program's by a relative error of at most 0.0085.
The roundings to bfloat16 on the way count: a program that leaves them out, or rounds other values in their place, can miss the bound.
Values may be sent and summed in bfloat16 or wider, within the bound.
No kernel may reach another device: no remote copies, remote signals or barrier semaphores. Data moves between devices by JAX's collectives and lax.ppermute only.
A program may use at most 128 MiB of HBM per device.

v0:
```python
import math

import jax
import jax.numpy as jnp
from jax import lax
from jax.sharding import PartitionSpec as P

HEADS = 8
GROUPS = 32


def spread_2(value, axis, source):
    kept = jnp.where(lax.axis_index(axis) == source, value, 0).astype(value.dtype)
    return lax.psum(kept, axis)


def shifted(block, axis, distance):
    devices = range(lax.axis_size(axis))
    route = [(i - distance, i) for i in devices if i - distance in devices]
    return lax.ppermute(block, axis, route)


def with_halo(value, sides, width):
    for axis, dim in sides:
        size, length = (lax.axis_size(axis), value.shape[dim])
        up = [(i, (i + 1) % size) for i in range(size - 1)]
        down = [(j, i) for i, j in up]
        last = lax.slice_in_dim(value, length - width, length, axis=dim)
        leading = lax.slice_in_dim(value, 0, width, axis=dim)
        before = lax.ppermute(last, axis, up)
        after = lax.ppermute(leading, axis, down)
        value = jnp.concatenate([before, value, after], axis=dim)
    return value


def layer_normed(values, gain_vec):
    floated = values.astype(jnp.float32)
    centre = floated - jnp.mean(floated, axis=-1, keepdims=True)
    spread = jnp.mean(centre * centre, axis=-1, keepdims=True)
    return (centre * lax.rsqrt(spread + 1e-05) * gain_vec.astype(jnp.float32)).astype(jnp.bfloat16)


def attend_frames(queries, key_set, value_set, factor):
    lead_keys = key_set[0]
    lead_values = value_set[0]

    def single(operands):
        frame_queries, frame_keys, frame_values = operands
        all_keys = jnp.concatenate([lead_keys, frame_keys], axis=0)
        all_values = jnp.concatenate([lead_values, frame_values], axis=0)
        scores = (
            jnp.einsum("qhd,khd->hqk", frame_queries, all_keys, preferred_element_type=jnp.float32)
            * factor
        )
        highest = jnp.max(scores, axis=-1, keepdims=True)
        raised = jnp.exp(scores - highest)
        totals = jnp.sum(raised, axis=-1)
        summed = jnp.einsum(
            "hqk,khd->qhd",
            raised.astype(jnp.bfloat16),
            all_values,
            preferred_element_type=jnp.float32,
        )
        return (summed / jnp.transpose(totals)[:, :, None]).astype(jnp.bfloat16)

    return lax.map(single, (queries, key_set[1:], value_set[1:]))


def body(latents, ln_gain, q_weight, k_weight, v_weight, o_weight, gn_gain, conv_weight, conv_bias):
    frames, row_count, col_count, channels = latents.shape
    tok_shard = row_count * col_count
    head_dim = channels // HEADS
    factor = 1.0 / math.sqrt(head_dim)
    tokens = latents.reshape(frames * tok_shard, channels)
    kv_weight = jnp.concatenate([k_weight, v_weight], axis=1)
    normed = layer_normed(tokens, ln_gain)
    queries = jnp.dot(normed, q_weight, preferred_element_type=jnp.float32).astype(jnp.bfloat16)
    queries = queries.reshape(frames, tok_shard, channels)
    paired = jnp.dot(normed, kv_weight, preferred_element_type=jnp.float32).astype(jnp.bfloat16)
    paired = paired.reshape(frames, tok_shard, 2 * channels)
    leading = spread_2(paired[0], "frame", 0)
    earlier = shifted(paired[frames - 1], "frame", 1)
    earlier = jnp.where(lax.axis_index("frame") == 0, paired[0], earlier)
    stacked = jnp.concatenate([leading[None], earlier[None], paired[: frames - 1]], axis=0)
    sent_queries = queries.reshape(frames, tok_shard, 1, HEADS, head_dim)
    sent_pairs = stacked.reshape(frames + 1, tok_shard, 2, HEADS, head_dim)
    got_queries, got_pairs = (
        lax.all_to_all(sent_queries, "row", split_axis=3, concat_axis=1, tiled=True),
        lax.all_to_all(sent_pairs, "row", split_axis=3, concat_axis=1, tiled=True),
    )
    head_results = attend_frames(
        got_queries[:, :, 0], got_pairs[:, :, 0], got_pairs[:, :, 1], factor
    )
    returned = lax.all_to_all(head_results, "row", split_axis=1, concat_axis=2, tiled=True)
    attended = returned.reshape(frames * tok_shard, channels)
    mixed = jnp.dot(attended, o_weight, preferred_element_type=jnp.float32)
    updated = (tokens.astype(jnp.float32) + mixed).astype(jnp.bfloat16)
    group_width = channels // GROUPS
    grouped = updated.astype(jnp.float32).reshape(frames, tok_shard, GROUPS, group_width)
    sum_parts = jnp.sum(grouped, axis=(1, 3))
    square_parts = jnp.sum(grouped * grouped, axis=(1, 3))
    group_sum, group_square = lax.psum((sum_parts, square_parts), "row")
    counted = tok_shard * lax.axis_size("row") * group_width
    group_mean = group_sum / counted
    group_var = group_square / counted - group_mean * group_mean
    scaled = (grouped - group_mean[:, None, :, None]) * lax.rsqrt(group_var + 1e-05)[
        :, None, :, None
    ]
    activated = jax.nn.silu(
        scaled.reshape(frames, tok_shard, channels) * gn_gain.astype(jnp.float32)
    )
    activated = activated.astype(jnp.bfloat16).reshape(frames, row_count, col_count, channels)
    padded = with_halo(activated, (("row", 1),), 1)
    padded = jnp.pad(padded, ((0, 0), (0, 0), (1, 1), (0, 0)))
    convolved = jnp.zeros((frames * tok_shard, channels), jnp.float32)
    for row_off in range(3):
        for col_off in range(3):
            window = padded[
                :, row_off : row_off + row_count, col_off : col_off + col_count, :
            ].reshape(frames * tok_shard, channels)
            convolved = convolved + jnp.dot(
                window, conv_weight[row_off, col_off], preferred_element_type=jnp.float32
            )
    output = updated.astype(jnp.float32) + convolved + conv_bias.astype(jnp.float32)
    return output.astype(jnp.bfloat16).reshape(frames, row_count, col_count, channels)


def solution(mesh):
    in_specs = (P("frame", "row", None, None), P(), P(), P(), P(), P(), P(), P(), P())
    out_specs = P("frame", "row", None, None)
    return jax.shard_map(body, mesh=mesh, in_specs=in_specs, out_specs=out_specs, check_vma=False)
```

profile of v0, /device:TPU:0, one launch (start us, length us, event | category | flops | bytes accessed | tf_op | source)
XLA Modules:
  0.0 480.2 jit_solution(6280379146752800633)
XLA Ops:
  6.5 1.9 convert_reduce_fusion
  10.4 2.6 convolution_convert_fusion
  13.0 1.5 copy-done.8
  15.5 3.2 collective-permute-start
  18.7 2.4 copy.41
  21.1 1.9 convolution_convert_fusion.1
  23.0 4.3 reshape_reshape.3
  27.3 4.8 %all-to-all-start.1 = ((bf16[4,512,1,8,40]{1,0,4,2,3:T(4,128)(2,1)}), bf16[4,512,1,8,40]{1,0,4,2,3:T(4,128)(2,1)}, u32[]{:S(2)}, u32[]{:S(2)}) async-start(bf16[4,512,1,8,40]{1,0,4,2,3:T(4,128)(2,1)} %bitcast.142), calls=%async_computation.1 | async-start | bytes 2621440 | tf_op jit(solution)/shard_map/all_to_all | solution.py:88
  32.1 1.5 slice.132
  33.6 5.7 %concatenate.31 = bf16[3,512,2,8,40]{1,0,4,3,2:T(4,128)(2,1)S(1)} reshape(bf16[1536,640]{0,1:T(8,128)(2,1)} %slice.132) | data formatting | bytes 3932160 | tf_op jit(solution)/shard_map/concatenate | solution.py:84
  39.3 1.2 broadcast_select_fusion
  40.5 2.3 copy.42
  42.8 73.9 %all-reduce.4.cloned.1.call-done = bf16[1,512,2,8,40]{1,0,4,3,2:T(2,128)(2,1)} async-done(((bf16[1,512,2,8,40]{1,0,4,3,2:T(2,128)(2,1)}), bf16[1,512,2,8,40]{1,0,4,3,2:T(2,128)(2,1)}) %all-reduce.4.cloned.1.call-update) | async-done | bytes 655376 | tf_op jit(solution)/shard_map/psum | solution.py:14
  116.7 5.8 %pad_maximum_fusion = bf16[5,512,2,8,40]{1,0,4,3,2:T(8,128)(2,1)S(1)} fusion(bf16[3,512,2,8,40]{1,0,4,3,2:T(4,128)(2,1)S(1)} %concatenate.31, bf16[1,512,2,8,40]{1,0,4,3,2:T(2,128)(2,1)} %copy.42, bf16[1,512,2,8,40]{1,0,4,3,2:T(2,128)(2,1)} %all-reduce.4.cloned.1.call-done), kind=kLoop, calls=%fused_computation.27 | loop fusion | flops 9830400 | bytes 6553600 | tf_op jit(solution)/shard_map/concatenate | solution.py:84
  122.5 3.0 copy.43
  125.6 4.5 all-to-all-start
  130.1 3.7 copy.46
  133.8 4.4 squeeze.52
  138.2 29.6 %all-to-all-done = bf16[5,512,2,8,40]{1,4,2,0,3:T(8,128)(2,1)S(1)} async-done(((bf16[5,512,2,8,40]{1,4,2,0,3:T(8,128)(2,1)}), bf16[5,512,2,8,40]{1,4,2,0,3:T(8,128)(2,1)S(1)}, u32[]{:S(2)}, u32[]{:S(2)}) %all-to-all-start) | async-done | bytes 3276832 | tf_op jit(solution)/shard_map/all_to_all | solution.py:89
  167.7 5.0 %copy.44 = bf16[5,2,512,2,4,40]{2,1,5,4,3,0:T(2,128)(2,1)} copy(bf16[5,2,512,2,4,40]{2,5,3,0,4,1:T(8,128)(2,1)S(1)} %bitcast.128) | data formatting | bytes 6553600 | tf_op jit(solution)/shard_map/all_to_all | solution.py:89
  172.8 7.3 %all_to_all.38 = bf16[5,1024,2,4,40]{1,4,3,2,0:T(8,128)(2,1)S(1)} reshape(bf16[5,2,512,2,4,40]{2,1,5,4,3,0:T(2,128)(2,1)} %copy.44) | data formatting | bytes 6553600 | tf_op jit(solution)/shard_map/all_to_all | solution.py:89
  180.1 1.9 slice_bitcast_fusion
  182.9 184.5 %while.10 = (s32[]{:T(128)}, bf16[4,1024,4,40]{1,3,2,0:T(8,128)(2,1)}, bf16[4,1024,4,40]{1,3,2,0:T(8,128)(2,1)}, bf16[1024,4,40]{0,2,1:T(8,128)(2,1)}, bf16[4,10...) while((s32[]{:T(128)}, ...), condition=%wide.region_6.7_spmd, body=%wide.region_3.6_spmd.sunk | while | flops 1412227072 | bytes 105333880 | solution.py:66
  183.1 1.1 dynamic-slice_bitcast_fusion.3
  184.2 16.7 %multiply_reduce_fusion.4 = (f32[4,1024]{1,0:T(4,128)S(1)}, f32[4,1024,2048]{2,1,0:T(8,128)}) fusion(bf16[1024,4,40]{0,2,1:T(8,128)(2,1)S(1)} %get-tuple-element.130, bf16[1024,4,40]{0,2,1:T(8,128)(2,1)} %get-tuple-element.156, bf16[4,1024,4,40]{1,3,2,0:T(8,128)(2,1)} %get-tuple-element.154, s32[]{:T(128)} %get-tuple-element.142), kind=kOutput, calls=%fused_computation.1.clone.1 | convolution fusion | flops 689172480 | bytes 34554368 | tf_op jit(solution)/shard_map/while/body/eval_jaxpr/qhd,khd->hqk/dot_general | solution.py:52
  201.0 14.0 %fusion.93 = f32[4,1024]{1,0:T(4,128)S(1)} fusion(f32[4,1024,2048]{2,1,0:T(8,128)} %get-tuple-element.131, f32[4,1024]{1,0:T(4,128)S(1)} %get-tuple-element.132), kind=kLoop, calls=%fused_computation.2.clone.1 | loop fusion | flops 25161728 | bytes 33587200 | tf_op jit(solution)/shard_map/while/body/eval_jaxpr/reduce_sum | solution.py:57
  215.0 14.2 %fusion.94 = bf16[4,1024,4,40]{1,3,2,0:T(8,128)(2,1)} fusion(bf16[4,1024,4,40]{1,3,2,0:T(8,128)(2,1)} %get-tuple-element.143, s32[]{:T(128)} %get-tuple-element.142, f32[4,1024,2048]{2,1,0:T(8,128)} %get-tuple-element.131, f32[4,1024]{1,0:T(4,128)S(1)} %get-tuple-element.132, bf16[1024,4,40]{0,2,1:T(8,128)(2,1)S(1)} %get-tuple-element.133, ...), kind=kOutput, calls=%fused_computation.9.clone.1 | convolution fusion | flops 697892864 | bytes 34570752 | tf_op jit(solution)/shard_map/while/body/eval_jaxpr/hqk,khd->qhd/dot_general | solution.py:58
  229.2 1.1 dynamic-slice_bitcast_fusion.3
  230.3 16.7 %multiply_reduce_fusion.4 = (f32[4,1024]{1,0:T(4,128)S(1)}, f32[4,1024,2048]{2,1,0:T(8,128)}) fusion(bf16[1024,4,40]{0,2,1:T(8,128)(2,1)S(1)} %get-tuple-element.130, bf16[1024,4,40]{0,2,1:T(8,128)(2,1)} %get-tuple-element.156, bf16[4,1024,4,40]{1,3,2,0:T(8,128)(2,1)} %get-tuple-element.154, s32[]{:T(128)} %get-tuple-element.142), kind=kOutput, calls=%fused_computation.1.clone.1 | convolution fusion | flops 689172480 | bytes 34554368 | tf_op jit(solution)/shard_map/while/body/eval_jaxpr/qhd,khd->hqk/dot_general | solution.py:52
  247.0 14.0 %fusion.93 = f32[4,1024]{1,0:T(4,128)S(1)} fusion(f32[4,1024,2048]{2,1,0:T(8,128)} %get-tuple-element.131, f32[4,1024]{1,0:T(4,128)S(1)} %get-tuple-element.132), kind=kLoop, calls=%fused_computation.2.clone.1 | loop fusion | flops 25161728 | bytes 33587200 | tf_op jit(solution)/shard_map/while/body/eval_jaxpr/reduce_sum | solution.py:57
  261.1 14.2 %fusion.94 = bf16[4,1024,4,40]{1,3,2,0:T(8,128)(2,1)} fusion(bf16[4,1024,4,40]{1,3,2,0:T(8,128)(2,1)} %get-tuple-element.143, s32[]{:T(128)} %get-tuple-element.142, f32[4,1024,2048]{2,1,0:T(8,128)} %get-tuple-element.131, f32[4,1024]{1,0:T(4,128)S(1)} %get-tuple-element.132, bf16[1024,4,40]{0,2,1:T(8,128)(2,1)S(1)} %get-tuple-element.133, ...), kind=kOutput, calls=%fused_computation.9.clone.1 | convolution fusion | flops 697892864 | bytes 34570752 | tf_op jit(solution)/shard_map/while/body/eval_jaxpr/hqk,khd->qhd/dot_general | solution.py:58
  275.2 1.1 dynamic-slice_bitcast_fusion.3
  276.4 16.7 %multiply_reduce_fusion.4 = (f32[4,1024]{1,0:T(4,128)S(1)}, f32[4,1024,2048]{2,1,0:T(8,128)}) fusion(bf16[1024,4,40]{0,2,1:T(8,128)(2,1)S(1)} %get-tuple-element.130, bf16[1024,4,40]{0,2,1:T(8,128)(2,1)} %get-tuple-element.156, bf16[4,1024,4,40]{1,3,2,0:T(8,128)(2,1)} %get-tuple-element.154, s32[]{:T(128)} %get-tuple-element.142), kind=kOutput, calls=%fused_computation.1.clone.1 | convolution fusion | flops 689172480 | bytes 34554368 | tf_op jit(solution)/shard_map/while/body/eval_jaxpr/qhd,khd->hqk/dot_general | solution.py:52
  293.1 14.0 %fusion.93 = f32[4,1024]{1,0:T(4,128)S(1)} fusion(f32[4,1024,2048]{2,1,0:T(8,128)} %get-tuple-element.131, f32[4,1024]{1,0:T(4,128)S(1)} %get-tuple-element.132), kind=kLoop, calls=%fused_computation.2.clone.1 | loop fusion | flops 25161728 | bytes 33587200 | tf_op jit(solution)/shard_map/while/body/eval_jaxpr/reduce_sum | solution.py:57
  307.2 14.2 %fusion.94 = bf16[4,1024,4,40]{1,3,2,0:T(8,128)(2,1)} fusion(bf16[4,1024,4,40]{1,3,2,0:T(8,128)(2,1)} %get-tuple-element.143, s32[]{:T(128)} %get-tuple-element.142, f32[4,1024,2048]{2,1,0:T(8,128)} %get-tuple-element.131, f32[4,1024]{1,0:T(4,128)S(1)} %get-tuple-element.132, bf16[1024,4,40]{0,2,1:T(8,128)(2,1)S(1)} %get-tuple-element.133, ...), kind=kOutput, calls=%fused_computation.9.clone.1 | convolution fusion | flops 697892864 | bytes 34570752 | tf_op jit(solution)/shard_map/while/body/eval_jaxpr/hqk,khd->qhd/dot_general | solution.py:58
  321.3 1.1 dynamic-slice_bitcast_fusion.3
  322.4 16.7 %multiply_reduce_fusion.4 = (f32[4,1024]{1,0:T(4,128)S(1)}, f32[4,1024,2048]{2,1,0:T(8,128)}) fusion(bf16[1024,4,40]{0,2,1:T(8,128)(2,1)S(1)} %get-tuple-element.130, bf16[1024,4,40]{0,2,1:T(8,128)(2,1)} %get-tuple-element.156, bf16[4,1024,4,40]{1,3,2,0:T(8,128)(2,1)} %get-tuple-element.154, s32[]{:T(128)} %get-tuple-element.142), kind=kOutput, calls=%fused_computation.1.clone.1 | convolution fusion | flops 689172480 | bytes 34554368 | tf_op jit(solution)/shard_map/while/body/eval_jaxpr/qhd,khd->hqk/dot_general | solution.py:52
  339.2 14.0 %fusion.93 = f32[4,1024]{1,0:T(4,128)S(1)} fusion(f32[4,1024,2048]{2,1,0:T(8,128)} %get-tuple-element.131, f32[4,1024]{1,0:T(4,128)S(1)} %get-tuple-element.132), kind=kLoop, calls=%fused_computation.2.clone.1 | loop fusion | flops 25161728 | bytes 33587200 | tf_op jit(solution)/shard_map/while/body/eval_jaxpr/reduce_sum | solution.py:57
  353.2 14.2 %fusion.94 = bf16[4,1024,4,40]{1,3,2,0:T(8,128)(2,1)} fusion(bf16[4,1024,4,40]{1,3,2,0:T(8,128)(2,1)} %get-tuple-element.143, s32[]{:T(128)} %get-tuple-element.142, f32[4,1024,2048]{2,1,0:T(8,128)} %get-tuple-element.131, f32[4,1024]{1,0:T(4,128)S(1)} %get-tuple-element.132, bf16[1024,4,40]{0,2,1:T(8,128)(2,1)S(1)} %get-tuple-element.133, ...), kind=kOutput, calls=%fused_computation.9.clone.1 | convolution fusion | flops 697892864 | bytes 34570752 | tf_op jit(solution)/shard_map/while/body/eval_jaxpr/hqk,khd->qhd/dot_general | solution.py:58
  367.4 7.3 %copy.47 = bf16[4,1024,4,40]{3,2,0,1:T(4,128)(2,1)} copy(bf16[4,1024,4,40]{1,3,2,0:T(8,128)(2,1)} %get-tuple-element.42) | data formatting | bytes 2621440 | tf_op jit(solution)/shard_map/while | solution.py:66
  374.7 8.8 %reshape.120 = bf16[2,2,163840]{2,1,0:T(2,128)(2,1)} reshape(bf16[1024,4,4,40]{3,2,1,0:T(4,128)(2,1)} %bitcast.126) | data formatting | bytes 2621440
  383.4 4.0 all-to-all-start.2
  387.4 1.9 copy.49
  389.4 13.8 %all-to-all-done.2 = bf16[2,2,163840]{2,1,0:T(2,128)(2,1)S(1)} async-done(((bf16[2,2,163840]{2,1,0:T(2,128)(2,1)}), bf16[2,2,163840]{2,1,0:T(2,128)(2,1)S(1)}, u32[]{:S(2)}, u32[]{:S(2)}) %all-to-all-start.2) | async-done | bytes 1310752 | tf_op jit(solution)/shard_map/all_to_all | solution.py:94
  403.2 8.0 %reshape.121 = bf16[1024,4,4,40]{3,2,1,0:T(4,128)(2,1)} reshape(bf16[2,2,163840]{2,1,0:T(2,128)(2,1)S(1)} %all-to-all-done.2) | data formatting | bytes 2621440
  411.2 6.7 %copy.48 = bf16[4,2,512,4,40]{2,0,4,3,1:T(4,128)(2,1)S(1)} copy(bf16[4,2,512,4,40]{4,3,0,2,1:T(4,128)(2,1)} %bitcast.127) | data formatting | bytes 2621440 | tf_op jit(solution)/shard_map/all_to_all | solution.py:94
  418.3 1.4 copy-done.7
  420.6 2.9 reshape.109
  423.5 2.3 copy.50
  425.8 2.7 fusion.71
  428.7 4.9 %all-reduce.1 = (f32[4,32]{1,0:T(4,128)S(1)}, f32[4,32]{1,0:T(4,128)S(1)}) all-reduce(f32[4,32]{1,0:T(4,128)S(1)} %copy.52, f32[4,32]{1,0:T(4,128)S(1)} %copy.51), channel_id=1, replica_groups=mesh['frame'=16,'row'=2] {'row'}, use_global_device_ids=true, to_apply=%region_10.11 | all-reduce | flops 256 | bytes 2048 | tf_op jit(solution)/shard_map/psum | solution.py:102
  434.0 2.8 multiply_convert_fusion
  436.9 1.1 copy-done.4
  438.0 2.2 collective-permute-start.1
  440.3 1.5 collective-permute-start.2
  441.8 2.0 sub.49
  443.8 3.4 copy.53
  447.2 2.0 mul.79
  449.2 3.5 copy.54
  452.7 2.2 fusion.43
  454.9 2.9 fusion.72
  464.9 1.4 convolution_add_fusion
  468.2 2.1 fusion.36
  470.3 2.5 copy.55
  (73 shorter events, 14.6 us)
Async XLA Ops:
  6.5 14.5 %copy-start = (bf16[320,320]{1,0:T(8,128)(2,1)S(1)}, bf16[320,320]{1,0:T(8,128)(2,1)}, u32[]{:S(2)}) copy-start(bf16[320,320]{1,0:T(8,128)(2,1)} %param.13) | copy-start | bytes 614404
  6.5 1.9 copy-start.2
  6.5 3.1 copy-start.14
  6.5 110.1 %all-reduce.4.cloned.1.call-start = ((), (), s32[]{:S(2)}) async-start(), calls=%async_computation.3 | async-start | bytes 2621440 | tf_op jit(solution)/shard_map/psum | solution.py:14
  13.0 1.5 copy-start.8
  15.5 23.8 %collective-permute-start = (bf16[512,640]{0,1:T(8,128)(2,1)}, bf16[512,640]{0,1:T(8,128)(2,1)}, u32[]{:S(2)}, u32[]{:S(2)}) collective-permute-start(bf16[512,640]{0,1:T(8,128)(2,1)} %get-tuple-element.70), channel_id=1, source_target_pairs={{0,2},{2,4},{4,6},{6,8},{8,10},{10,12},{12,14},{14,16},{16,18},{18... | collective-permute-start | bytes 1966088 | tf_op jit(solution)/shard_map/ppermute | solution.py:20
  23.0 9.1 %copy-start.9 = (bf16[2048,640]{0,1:T(8,128)(2,1)S(1)}, bf16[2048,640]{0,1:T(8,128)(2,1)}, u32[]{:S(2)}) copy-start(bf16[2048,640]{0,1:T(8,128)(2,1)} %copy-done.8) | copy-start | bytes 7864324
  27.3 98.3 %all-to-all-start.1 = ((bf16[4,512,1,8,40]{1,0,4,2,3:T(4,128)(2,1)}), bf16[4,512,1,8,40]{1,0,4,2,3:T(4,128)(2,1)}, u32[]{:S(2)}, u32[]{:S(2)}) async-start(bf16[4,512,1,8,40]{1,0,4,2,3:T(4,128)(2,1)} %bitcast.142), calls=%async_computation.1 | async-start | bytes 2621440 | tf_op jit(solution)/shard_map/all_to_all | solution.py:88
  125.6 42.2 %all-to-all-start = ((bf16[5,512,2,8,40]{1,4,2,0,3:T(8,128)(2,1)}), bf16[5,512,2,8,40]{1,4,2,0,3:T(8,128)(2,1)S(1)}, u32[]{:S(2)}, u32[]{:S(2)}) async-start(bf16[5,512,2,8,40]{1,4,2,0,3:T(8,128)(2,1)} %copy.43), calls=%async_computation | async-start | bytes 6553600 | tf_op jit(solution)/shard_map/all_to_all | solution.py:89
  201.0 14.0 %copy-start.6 = (bf16[1024,4,40]{0,2,1:T(8,128)(2,1)S(1)}, bf16[1024,4,40]{0,2,1:T(8,128)(2,1)}, u32[]{:S(2)}) copy-start(bf16[1024,4,40]{0,2,1:T(8,128)(2,1)} %get-tuple-element.153) | copy-start | bytes 983044 | tf_op jit(solution)/shard_map/while
  247.0 14.0 %copy-start.6 = (bf16[1024,4,40]{0,2,1:T(8,128)(2,1)S(1)}, bf16[1024,4,40]{0,2,1:T(8,128)(2,1)}, u32[]{:S(2)}) copy-start(bf16[1024,4,40]{0,2,1:T(8,128)(2,1)} %get-tuple-element.153) | copy-start | bytes 983044 | tf_op jit(solution)/shard_map/while
  293.1 14.0 %copy-start.6 = (bf16[1024,4,40]{0,2,1:T(8,128)(2,1)S(1)}, bf16[1024,4,40]{0,2,1:T(8,128)(2,1)}, u32[]{:S(2)}) copy-start(bf16[1024,4,40]{0,2,1:T(8,128)(2,1)} %get-tuple-element.153) | copy-start | bytes 983044 | tf_op jit(solution)/shard_map/while
  339.2 14.0 %copy-start.6 = (bf16[1024,4,40]{0,2,1:T(8,128)(2,1)S(1)}, bf16[1024,4,40]{0,2,1:T(8,128)(2,1)}, u32[]{:S(2)}) copy-start(bf16[1024,4,40]{0,2,1:T(8,128)(2,1)} %get-tuple-element.153) | copy-start | bytes 983044 | tf_op jit(solution)/shard_map/while
  383.4 4.0 copy-start.3
  383.4 19.7 %all-to-all-start.2 = ((bf16[2,2,163840]{2,1,0:T(2,128)(2,1)}), bf16[2,2,163840]{2,1,0:T(2,128)(2,1)S(1)}, u32[]{:S(2)}, u32[]{:S(2)}) async-start(bf16[2,2,163840]{2,1,0:T(2,128)(2,1)} %reshape.120), calls=%async_computation.2 | async-start | bytes 2621440 | tf_op jit(solution)/shard_map/all_to_all | solution.py:94
  387.4 1.9 copy-start.15
  411.2 7.1 %copy-start.13 = (bf16[320,320]{1,0:T(8,128)(2,1)S(1)}, bf16[320,320]{1,0:T(8,128)(2,1)}, u32[]{:S(2)}) copy-start(bf16[320,320]{1,0:T(8,128)(2,1)} %param.16) | copy-start | bytes 614404
  417.9 1.7 copy-start.7
  433.8 8.0 %copy-start.16 = (bf16[320]{0:T(512)(128)(2,1)S(1)}, bf16[320]{0:T(512)(128)(2,1)}, u32[]{:S(2)}) copy-start(bf16[320]{0:T(512)(128)(2,1)} %param.19) | copy-start | bytes 1924
  436.9 1.1 copy-start.4
  438.0 14.7 %collective-permute-start.1 = (bf16[4,1,32,320]{3,2,1,0:T(8,128)(2,1)S(1)}, bf16[4,1,32,320]{3,2,1,0:T(8,128)(2,1)S(1)}, u32[]{:S(2)}, u32[]{:S(2)}) collective-permute-start(bf16[4,1,32,320]{3,2,1,0:T(8,128)(2,1)S(1)} %get-tuple-element.79), channel_id=1, source_target_pairs={{0,1},{2,3},{4,5},{6,7},{8,9},{10,11},{12,13},{14,15},{16,17},{18,... | collective-permute-start | bytes 245768 | tf_op jit(solution)/shard_map/ppermute | solution.py:30
  440.3 12.4 %collective-permute-start.2 = (bf16[4,1,32,320]{3,2,1,0:T(8,128)(2,1)S(1)}, bf16[4,1,32,320]{3,2,1,0:T(8,128)(2,1)S(1)}, u32[]{:S(2)}, u32[]{:S(2)}) collective-permute-start(bf16[4,1,32,320]{3,2,1,0:T(8,128)(2,1)S(1)} %get-tuple-element.80), channel_id=1, source_target_pairs={{1,0},{3,2},{5,4},{7,6},{9,8},{11,10},{13,12},{15,14},{17,16},{19,... | collective-permute-start | bytes 245768 | tf_op jit(solution)/shard_map/ppermute | solution.py:31
  454.9 2.9 copy-start.12
  458.7 1.4 copy-start.5
  462.4 1.7 copy-start.10
  462.4 2.5 copy-start.11
  468.2 4.7 copy-start.1
Sparse Core Ops, SparseCore 0:
  21.2 95.4 all-reduce.3
where the time goes:
time: 487 us; the launch traced here: 480 us
  matrix products  139 us (29%)
  waiting for transfers between devices  117 us (24%)
  local copies, waits for them, and re-layouts  108 us (22%)
  other arithmetic  76 us (16%)
  starting transfers between devices  20.2 us (4%)
  between operations  14.2 us (3%)
  blocking collectives  4.93 us (1%)
    psum x1, waiting for transfers between devices, spread_2(): return lax.psum(kept, axis)  73.9 us
    dot_general x4, matrix products, single(): jnp.einsum('qhd,khd->hqk', frame_queries, all_keys, preferred_element_typ...  66.9 us
    dot_general x4, matrix products, single(): jnp.einsum('hqk,khd->qhd', raised.astype(jnp.bfloat16), all_values, prefe...  56.7 us
    reduce_sum x4, other arithmetic, single(): totals = jnp.sum(raised, axis=-1)  56.1 us
    all_to_all x1, waiting for transfers between devices, body(): lax.all_to_all(sent_pairs, 'row', split_axis=3, concat_axis=1, tiled=True)  29.6 us
    unnamed x35, local copies, waits for them, and re-layouts  23.3 us
    all_to_all x1, waiting for transfers between devices, body(): lax.all_to_all(head_results, 'row', split_axis=1, concat_axis=2, tiled=True)  13.8 us
    concatenate x4, local copies, waits for them, and re-layouts, body(): jnp.concatenate([leading[None], earlier[None], paired[:frames - 1]], axis=0)  13.4 us
  transfers between devices with their start and end apart: 7, of which 3 were waited for; matrix products, arithmetic and copies ran while one was open for 10% of the time, Pallas kernels for 0%

commit v1 on v0

v1 whole, which is shorter than its diff:
```python
import functools
import math

import jax
import jax.numpy as jnp
import numpy as np
from jax import lax
from jax.experimental import pallas as pl
from jax.experimental.pallas import tpu as pltpu
from jax.sharding import PartitionSpec as P

HEADS = 8
GROUPS = 32
KPAD = 64
VPAD = 48
BF16, F32 = jnp.bfloat16, jnp.float32
VMEM_BYTES = 50 * 2**20


def head_spread(channels, pad):
    dim = channels // HEADS
    out = np.zeros((HEADS * pad, channels), np.float32)
    for c in range(channels):
        out[c // dim * pad + c % dim, c] = 1.0
    return jnp.asarray(out, BF16)


def nt(a, b):
    return lax.dot_general(a, b, (((1,), (1,)), ((), ())), preferred_element_type=F32)


def normed_of(x, gain):
    floated = x.astype(F32)
    centre = floated - jnp.mean(floated, axis=-1, keepdims=True)
    spread = jnp.mean(centre * centre, axis=-1, keepdims=True)
    return (centre * lax.rsqrt(spread + 1e-05) * gain).astype(BF16)


def params(grid_rank=1):
    return pltpu.CompilerParams(
        vmem_limit_bytes=VMEM_BYTES, dimension_semantics=("arbitrary",) * grid_rank
    )


def query_kernel(x_ref, g_ref, wq_ref, wk_ref, wv_ref, wo_ref, ek_ref, ev_ref,
                 qt_ref, wkp_ref, wvt_ref, wop_ref, wqt_ref):
    @pl.when(pl.program_id(0) == 0)
    def _():
        ek, ev = ek_ref[...], ev_ref[...]
        wqt_ref[...] = nt(ek, wq_ref[...]).astype(BF16)
        wkp_ref[...] = nt(wk_ref[...], ek).astype(BF16)
        wvt_ref[...] = nt(ev, wv_ref[...]).astype(BF16)
        wop_ref[...] = jnp.dot(ev, wo_ref[...], preferred_element_type=F32).astype(BF16)

    normed = normed_of(x_ref[0], g_ref[...].astype(F32))
    qt_ref[0] = nt(wqt_ref[...], normed).astype(BF16)


def make_queries(x, gain, wq, wk, wv, wo):
    frames, tok, ch = x.shape
    ek, ev = head_spread(ch, KPAD), head_spread(ch, VPAD)
    nk, nv = HEADS * KPAD, HEADS * VPAD
    whole = lambda shape: pl.BlockSpec(shape, lambda i: (0,) * len(shape))
    return pl.pallas_call(
        query_kernel,
        grid=(frames,),
        in_specs=[pl.BlockSpec((1, tok, ch), lambda i: (i, 0, 0)), whole((1, ch))]
        + [whole((ch, ch))] * 4 + [whole((nk, ch)), whole((nv, ch))],
        out_specs=[pl.BlockSpec((1, nk, tok), lambda i: (i, 0, 0)),
                   whole((ch, nk)), whole((nv, ch)), whole((nv, ch))],
        out_shape=[jax.ShapeDtypeStruct((frames, nk, tok), BF16),
                   jax.ShapeDtypeStruct((ch, nk), BF16),
                   jax.ShapeDtypeStruct((nv, ch), BF16),
                   jax.ShapeDtypeStruct((nv, ch), BF16)],
        scratch_shapes=[pltpu.VMEM((nk, ch), BF16)],
        compiler_params=params(),
        cost_estimate=pl.CostEstimate(flops=3_000_000_000, bytes_accessed=6_000_000, transcendentals=0),
        name="queries",
    )(x, gain, wq, wk, wv, wo, ek, ev)


def flash_kernel(cfg, *refs):
    segs, once, first, last, select, rows, pair = cfg
    refs = list(refs)
    take = lambda n: [refs.pop(0) for _ in range(n)]
    (flag_ref,) = take(1)
    seg_refs = take(segs * (2 if select else 1))
    qt_ref, g_ref, wkp_ref, wvt_ref = take(4)
    if not first:
        m_in, acc_in = take(2)
    if last:
        x_ref, wop_ref = take(2)
        upd_ref, edge_ref, stat_ref = take(3)
    else:
        m_out, acc_out = take(2)
    k_ref, vt_ref, s_ref = take(3)
    att_ref = refs.pop(0) if last else None
    tok = qt_ref.shape[2]
    ch = g_ref.shape[1]
    dim = ch // HEADS
    factor = math.log2(math.e) / math.sqrt(dim)

    def make_kv():
        at = 0
        gain = g_ref[...].astype(F32)
        for i in range(segs):
            x = seg_refs[i][0]
            if select:
                x = jnp.where(flag_ref[0] == 0, seg_refs[segs + i][0], x)
            n = x.shape[0]
            normed = normed_of(x, gain)
            k_ref[at:at + n, :] = jnp.dot(normed, wkp_ref[...], preferred_element_type=F32).astype(BF16)
            vt = nt(wvt_ref[...], normed).astype(BF16)
            for h in range(HEADS):
                vt_ref[h * VPAD:(h + 1) * VPAD, at:at + n] = vt[h * VPAD:(h + 1) * VPAD]
            at += n

    if once:
        pl.when(pl.program_id(0) == 0)(make_kv)
    else:
        make_kv()

    zeros = jnp.zeros((KPAD, tok), BF16)
    row = lax.broadcasted_iota(jnp.int32, (VPAD, vt_ref.shape[1]), 0)

    def scores(h):
        own = qt_ref[0, h * KPAD:(h + 1) * KPAD, :]
        both = jnp.concatenate([own, zeros] if h % 2 == 0 else [zeros, own], axis=0)
        lanes = h // 2 * 2 * KPAD
        s_ref[h % 2] = jnp.dot(k_ref[:, lanes:lanes + 2 * KPAD], both, preferred_element_type=F32)

    scores(0)
    for h in range(HEADS):
        if h + 1 < HEADS:
            scores(h + 1)
        s = s_ref[h % 2]
        top = jnp.max(s, axis=0, keepdims=True)
        if not first:
            old = m_in[0, h:h + 1, :]
            top = jnp.maximum(top, old)
        weights = jnp.exp2((s - top) * factor).astype(BF16)
        values = vt_ref[h * VPAD:(h + 1) * VPAD, :]
        values = jnp.where(row == dim, jnp.ones_like(values), values)
        part = jnp.dot(values, weights, preferred_element_type=F32)
        if not first:
            part = part + acc_in[0, h * VPAD:(h + 1) * VPAD, :] * jnp.exp2((old - top) * factor)
        if last:
            att_ref[h * VPAD:(h + 1) * VPAD, :] = (part / part[dim:dim + 1]).astype(BF16)
        else:
            m_out[0, h:h + 1, :] = top
            acc_out[0, h * VPAD:(h + 1) * VPAD, :] = part

    if last:
        mixed = lax.dot_general(att_ref[...], wop_ref[...], (((0,), (0,)), ((), ())),
                                preferred_element_type=F32)
        updated = (x_ref[0].astype(F32) + mixed).astype(BF16)
        upd_ref[0] = updated
        floated = updated.astype(F32)
        cols = tok // rows
        sums = jnp.sum(floated, axis=0, keepdims=True)
        squares = jnp.sum(floated * floated, axis=0, keepdims=True)
        which = lax.broadcasted_iota(jnp.int32, (8, ch), 0)
        stats = jnp.where(which == 0, sums, jnp.where(which == 1, squares, 0.0))
        stat_ref[0] = stats
        if pair:
            edge_ref[0, 0:cols] = jnp.where(flag_ref[1] == 0, floated[tok - cols:], floated[:cols])
            edge_ref[0, cols:cols + 8] = stats
        else:
            edge_ref[0, 0:cols] = floated[:cols]
            edge_ref[0, cols:2 * cols] = floated[tok - cols:]


def flash(name, flags, start, count, segments, qt, gain, wkp, wvt, state=None, once=False,
          select=None, last=None, rows=None, pair=True):
    frames, nk, tok = qt.shape
    ch = gain.shape[1]
    nv = HEADS * VPAD
    whole = lambda shape: pl.BlockSpec(shape, lambda i: (0,) * len(shape))
    seg_specs, seg_args = [], []
    for arr, block in list(segments) + list(select or []):
        seg_specs.append(pl.BlockSpec((1,) + arr.shape[1:], functools.partial(lambda b, i: (b(i), 0, 0), block)))
        seg_args.append(arr)
    keys = sum(arr.shape[1] for arr, _ in segments)
    frame = lambda shape: pl.BlockSpec((1,) + shape, lambda i: (i + start, 0, 0))
    first = state is None
    in_specs = [pl.BlockSpec(memory_space=pltpu.SMEM)] + seg_specs + [
        frame((nk, tok)), whole((1, ch)), whole(wkp.shape), whole(wvt.shape)]
    args = [flags] + seg_args + [qt, gain, wkp, wvt]
    aliases = {}
    state_shapes = [jax.ShapeDtypeStruct((frames, HEADS, tok), F32), jax.ShapeDtypeStruct((frames, nv, tok), F32)]
    state_specs = [frame((HEADS, tok)), frame((nv, tok))]
    scratch = [pltpu.VMEM((keys, nk), BF16), pltpu.VMEM((nv, keys), BF16), pltpu.VMEM((2, keys, tok), F32)]
    if not first:
        if last is None:
            aliases = {len(args): 0, len(args) + 1: 1}
        in_specs += state_specs
        args += list(state)
    if last is None:
        out_shape, out_specs = state_shapes, state_specs
    else:
        x, wop = last
        cols = tok // rows
        in_specs += [frame((tok, ch)), whole(wop.shape)]
        args += [x, wop]
        edge = cols + 8 if pair else 2 * cols
        out_shape = [jax.ShapeDtypeStruct((count, tok, ch), BF16),
                     jax.ShapeDtypeStruct((count, edge, ch), F32),
                     jax.ShapeDtypeStruct((count, 8, ch), F32)]
        out_specs = [pl.BlockSpec((1,) + o.shape[1:], lambda i: (i, 0, 0)) for o in out_shape]
        scratch.append(pltpu.VMEM((nv, tok), BF16))
    cfg = (len(segments), once, first, last is not None, select is not None, rows, pair)
    scores = count * HEADS * keys * tok
    return pl.pallas_call(
        functools.partial(flash_kernel, cfg),
        grid=(count,),
        in_specs=in_specs,
        out_specs=out_specs,
        out_shape=out_shape,
        scratch_shapes=scratch,
        input_output_aliases=aliases,
        compiler_params=params(),
        cost_estimate=pl.CostEstimate(flops=scores * 1400, bytes_accessed=scores // 8, transcendentals=scores),
        name=name,
    )(*args)


def conv_kernel(cfg, flag_ref, upd_ref, top_ref, bot_ref, stat_ref, gn_ref, bias_ref, group_ref, w_ref,
                out_ref, act_ref):
    rows, cols, count, pair, bot_at = cfg
    tok, ch = upd_ref.shape[1:]
    stats = stat_ref[0]
    if pair:
        stats = stats + top_ref[0, cols:cols + 8]
    grouped = jnp.dot(stats, group_ref[...].astype(F32), precision=lax.Precision.HIGHEST,
                      preferred_element_type=F32) / count
    mean = grouped[0:1]
    var = grouped[1:2] - mean * mean
    scale = lax.rsqrt(var + 1e-05)
    gain = gn_ref[...].astype(F32)

    def activated(u):
        v = (u.astype(F32) - mean) * scale * gain
        return v / (1.0 + jnp.exp(-v))

    above = jnp.where(flag_ref[2] == 1, activated(top_ref[0, 0:cols]), 0.0)
    below = jnp.where(flag_ref[3] == 1, activated(bot_ref[0, bot_at:bot_at + cols]), 0.0)
    act_ref[0:cols] = above.astype(BF16)
    act_ref[cols:cols + tok] = activated(upd_ref[0]).astype(BF16)
    act_ref[cols + tok:2 * cols + tok] = below.astype(BF16)
    column = lax.broadcasted_iota(jnp.int32, (tok, ch), 0) % cols
    total = upd_ref[0].astype(F32) + bias_ref[...].astype(F32)
    for b in range(3):
        part = jnp.zeros((tok, ch), F32)
        for a in range(3):
            part += jnp.dot(act_ref[a * cols:a * cols + tok, :], w_ref[a, b], preferred_element_type=F32)
        if b == 0:
            part = jnp.where(column == 0, 0.0, pltpu.roll(part, 1, 0))
        if b == 2:
            part = jnp.where(column == cols - 1, 0.0, pltpu.roll(part, tok - 1, 0))
        total += part
    out_ref[0] = total.astype(BF16)


def conv(flags, upd, top, bot, bot_at, stats, gn, bias, group, weight, rows, pair, count):
    frames, tok, ch = upd.shape
    cols = tok // rows
    per = lambda a: pl.BlockSpec((1,) + a.shape[1:], lambda i: (i, 0, 0))
    whole = lambda a: pl.BlockSpec(a.shape, lambda i: (0,) * a.ndim)
    return pl.pallas_call(
        functools.partial(conv_kernel, (rows, cols, count, pair, bot_at)),
        grid=(frames,),
        in_specs=[pl.BlockSpec(memory_space=pltpu.SMEM), per(upd), per(top), per(bot), per(stats),
                  whole(gn), whole(bias), whole(group), whole(weight)],
        out_specs=per(upd),
        out_shape=jax.ShapeDtypeStruct(upd.shape, BF16),
        scratch_shapes=[pltpu.VMEM((tok + 2 * cols, ch), BF16)],
        compiler_params=params(),
        cost_estimate=pl.CostEstimate(flops=frames * tok * ch * ch * 40, bytes_accessed=4_000_000, transcendentals=0),
        name="conv",
    )(flags, upd, top, bot, stats, gn, bias, group, weight)


def spread_first(value, axis):
    size = lax.axis_size(axis)
    me = lax.axis_index(axis)
    stride = 1
    while stride * 2 < size:
        stride *= 2
    have = [0]
    while stride >= 1:
        route = [(i, i + stride) for i in have if i + stride < size]
        if route:
            got = lax.ppermute(value, axis, route)
            new = [j for _, j in route]
            value = jnp.where((me % (2 * stride)) == stride, got, value)
            have += new
        stride //= 2
    return value


def others(value, rows, axis=1):
    got = [lax.ppermute(value, "row", [(i, (i + k) % rows) for i in range(rows)]) for k in range(1, rows)]
    return got[0] if len(got) == 1 else jnp.concatenate(got, axis=axis)


def body(latents, ln_gain, q_weight, k_weight, v_weight, o_weight, gn_gain, conv_weight, conv_bias):
    frames, row_count, cols, ch = latents.shape
    tok = row_count * cols
    size, blocks = lax.axis_size("row"), lax.axis_size("frame")
    me, block = lax.axis_index("row"), lax.axis_index("frame")
    pair = size == 2
    x = latents.reshape(frames, tok, ch)
    gain = ln_gain.reshape(1, ch)
    flags = jnp.stack([block, me, (me > 0).astype(jnp.int32), (me < size - 1).astype(jnp.int32)]).astype(jnp.int32)

    last_own = x[frames - 1:]
    routes = [[(f * size + r, (f + 1) * size + (r + k) % size) for f in range(blocks - 1) for r in range(size)]
              for k in range(size)]
    lead = spread_first(x[0:1], "frame")
    side = others(x[0:frames - 1], size)
    came = [lax.ppermute(last_own, ("frame", "row"), route) for route in routes]
    prev_own = came[0]
    prev_side = came[1] if size == 2 else jnp.concatenate(came[1:], axis=1)
    lead_side = others(lead, size)

    qt, wkp, wvt, wop = make_queries(x, gain, q_weight, k_weight, v_weight, o_weight)
    common = (qt, gain, wkp, wvt)
    state = flash("own", flags, 1, frames - 1, [(x, lambda i: i)], *common)
    state = flash("side", flags, 1, frames - 1, [(side, lambda i: i)], *common, state=state)
    zero = lambda i: 0
    state0 = flash("prev", flags, 0, 1, [(prev_own, zero), (prev_side, zero)], *common,
                   select=[(x, zero), (side, zero)])
    state = [lax.dynamic_update_slice_in_dim(s, s0[0:1], 0, 0) for s, s0 in zip(state, state0)]
    half = frames // 2
    group = jnp.asarray(np.kron(np.eye(GROUPS), np.ones((ch // GROUPS,) * 2)), BF16)
    outs = []
    for start in (0, half):
        upd, edge, stats = flash("lead", flags, start, half, [(lead, zero), (lead_side, zero)], *common,
                                 state=state, once=True, last=(x, wop), rows=row_count, pair=pair)
        if pair:
            got = lax.ppermute(edge, "row", [(0, 1), (1, 0)])
            top, bot, bot_at = got, got, 0
        else:
            top = lax.ppermute(edge[:, cols:], "row", [(i, i + 1) for i in range(size - 1)])
            bot = lax.ppermute(edge[:, :cols], "row", [(i + 1, i) for i in range(size - 1)])
            bot_at = 0
            stats = lax.psum(stats, "row")
        outs.append(conv(flags, upd, top, bot, bot_at, stats, gn_gain.reshape(1, ch), conv_bias.reshape(1, ch),
                         group, conv_weight, row_count, pair, tok * size * (ch // GROUPS)))
    return jnp.concatenate(outs, axis=0).reshape(latents.shape)


def solution(mesh):
    in_specs = (P("frame", "row", None, None), P(), P(), P(), P(), P(), P(), P(), P())
    out_specs = P("frame", "row", None, None)
    return jax.shard_map(body, mesh=mesh, in_specs=in_specs, out_specs=out_specs, check_vma=False)
```

time: 487 us -> 129 us (0.26); the launches traced: 480 us -> 128 us
  matrix products: 139 us -> 0 us
  waiting for transfers between devices: 117 us -> 4.21 us
  local copies, waits for them, and re-layouts: 108 us -> 10.8 us
  Pallas kernels: 0 us -> 85.6 us
  other arithmetic: 76 us -> 5.66 us
  between operations: 14.2 us -> 0.28 us
  blocking collectives: 4.93 us -> 0 us
    dot_general x20 -> x0, matrix products: 139 us -> none  [the longest x4 66.9 us: single(): jnp.einsum('qhd,khd->hqk', frame_queries, all_keys, preferred_element_typ...]
    pallas_call x0 -> x8, Pallas kernels: none -> 85.6 us  [the longest x5 64.3 us: flash(): pl.pallas_call(functools.partial(flash_kernel, cfg), grid=(count,), in_sp...]
    psum x1 -> x0, waiting for transfers between devices: 73.9 us -> none  [spread_2(): return lax.psum(kept, axis)]
    reduce_sum x7 -> x0, other arithmetic: 61.8 us -> none  [the longest x4 56.1 us: single(): totals = jnp.sum(raised, axis=-1)]
    all_to_all x3 -> x0, waiting for transfers between devices: 43.4 us -> none  [the longest x1 29.6 us: body(): lax.all_to_all(sent_pairs, 'row', split_axis=3, concat_axis=1, tiled=True)]
    all_to_all x4 -> x0, local copies, waits for them, and re-layouts: 22.8 us -> none  [the longest x2 12.4 us: body(): lax.all_to_all(sent_pairs, 'row', split_axis=3, concat_axis=1, tiled=True)]
    unnamed x35 -> x36, local copies, waits for them, and re-layouts: 23.3 us -> 3.61 us
    ppermute x3 -> x10, starting transfers between devices: 6.96 us -> 21.4 us  [the longest x4 13.6 us: spread_first(): got = lax.ppermute(value, axis, route)]
  transfers between devices with their start and end apart: 7 -> 10, of which waited for: 3 -> 1; matrix products, arithmetic and copies ran while one was open for 10% -> 6% of each run, Pallas kernels for 0% -> 49%
where the time goes in v1:
time: 129 us; the launch traced here: 128 us
  Pallas kernels  85.6 us (66%)
  starting transfers between devices  21.4 us (17%)
  local copies, waits for them, and re-layouts  10.8 us (8%)
  other arithmetic  5.66 us (4%)
  waiting for transfers between devices  4.21 us (3%)
    pallas_call x5, Pallas kernels, flash(): pl.pallas_call(functools.partial(flash_kernel, cfg), grid=(count,), in_sp...  64.3 us
    pallas_call x2, Pallas kernels, conv(): pl.pallas_call(functools.partial(conv_kernel, (rows, cols, count, pair, b...  15 us
    ppermute x4, starting transfers between devices, spread_first(): got = lax.ppermute(value, axis, route)  13.6 us
    pallas_call x1, Pallas kernels, make_queries(): pl.pallas_call(query_kernel, grid=(frames,), in_specs=[pl.BlockSpec((1, t...  6.29 us
    ppermute x2, waiting for transfers between devices, others(): lax.ppermute(value, 'row', [(i, (i + k) % rows) for i in range(rows)])  4.19 us
    select_n x4, other arithmetic, spread_first(): value = jnp.where(me % (2 * stride) == stride, got, value)  4.17 us
    unnamed x36, local copies, waits for them, and re-layouts  3.61 us
    ppermute x2, starting transfers between devices, others(): lax.ppermute(value, 'row', [(i, (i + k) % rows) for i in range(rows)])  3 us
  transfers between devices with their start and end apart: 10, of which 1 were waited for; matrix products, arithmetic and copies ran while one was open for 6% of the time, Pallas kernels for 49%

profile of v1, /device:TPU:0, one launch (start us, length us, event | category | flops | bytes accessed | tf_op | source)
XLA Modules:
  0.0 128.0 jit_solution(6229840632999383913)
XLA Ops:
  0.0 2.1 %fusion = (bf16[1,16,32,320]{3,2,1,0:T(8,128)(2,1)}, bf16[1,16,32,320]{3,2,1,0:T(8,128)(2,1)S(1)}) fusion(bf16[4,16,32,320]{3,2,1,0:T(8,128)(2,1)} %param.12), kind=kLoop, calls=%fused_computation.8 | loop fusion | bytes 1310720 | tf_op jit(solution)/shard_map/slice | solution.py:316
  2.1 6.7 %collective-permute-start = (bf16[1,512,320]{2,1,0:T(8,128)(2,1)S(1)}, bf16[1,512,320]{2,1,0:T(8,128)(2,1)}, u32[]{:S(2)}, u32[]{:S(2)}) collective-permute-start(bf16[1,512,320]{2,1,0:T(8,128)(2,1)S(1)} %bitcast.16), channel_id=1, source_target_pairs={{0,16},{1,17}} | collective-permute-start | bytes 983048 | tf_op jit(solution)/shard_map/ppermute | solution.py:293
  8.7 1.3 %collective-permute-start.6 = (bf16[1,512,320]{2,1,0:T(8,128)(2,1)}, bf16[1,512,320]{2,1,0:T(8,128)(2,1)S(1)}, u32[]{:S(2)}, u32[]{:S(2)}) collective-permute-start(bf16[1,512,320]{2,1,0:T(8,128)(2,1)} %bitcast.7), channel_id=1, source_target_pairs={{0,2},{1,3},{2,4},{3,5},{4,6},{5,7},{6,8},{7,9},{8,10},{9,11},{10,... | collective-permute-start | bytes 983048 | tf_op jit(solution)/shard_map/ppermute | solution.py:321
  10.1 1.4 %collective-permute-start.7 = (bf16[1,512,320]{2,1,0:T(8,128)(2,1)}, bf16[1,512,320]{2,1,0:T(8,128)(2,1)S(1)}, u32[]{:S(2)}, u32[]{:S(2)}) collective-permute-start(bf16[1,512,320]{2,1,0:T(8,128)(2,1)} %bitcast.7), channel_id=1, source_target_pairs={{0,3},{1,2},{2,5},{3,4},{4,7},{5,6},{6,9},{7,8},{8,11},{9,10},{10,... | collective-permute-start | bytes 983048 | tf_op jit(solution)/shard_map/ppermute | solution.py:321
  11.5 0.0 copy-start.15
  11.5 0.0 copy-start.1
  11.5 0.0 copy-start.2
  11.5 0.0 copy-start.3
  11.5 0.0 copy-start.4
  11.5 0.0 slice-done
  11.6 1.4 %copy.18 = bf16[3,512,320]{1,2,0:T(8,128)(2,1)} copy(bf16[3,512,320]{2,1,0:T(8,128)(2,1)S(1)} %bitcast.15) | data formatting | bytes 1966080 | tf_op jit(solution)/shard_map/slice | solution.py:320
  12.9 1.4 %collective-permute-start.5 = (bf16[3,512,320]{1,2,0:T(8,128)(2,1)}, bf16[3,512,320]{1,2,0:T(8,128)(2,1)}, u32[]{:S(2)}, u32[]{:S(2)}) collective-permute-start(bf16[3,512,320]{1,2,0:T(8,128)(2,1)} %copy.18), channel_id=1, source_target_pairs={{0,1},{1,0},{2,3},{3,2},{4,5},{5,4},{6,7},{7,6},{8,9},{9,8},{10,11... | collective-permute-start | bytes 2949128 | tf_op jit(solution)/shard_map/ppermute | solution.py:302
  14.3 0.0 collective-permute-done
  14.3 0.9 broadcast_select_fusion
  15.2 3.3 %collective-permute-start.1 = (bf16[1,512,320]{2,1,0:T(8,128)(2,1)}, bf16[1,512,320]{2,1,0:T(8,128)(2,1)}, u32[]{:S(2)}, u32[]{:S(2)}) collective-permute-start(bf16[1,512,320]{2,1,0:T(8,128)(2,1)} %broadcast_select_fusion), channel_id=1, source_target_pairs={{0,8},{16,24},{1,9},{17,25}} | collective-permute-start | bytes 983048 | tf_op jit(solution)/shard_map/ppermute | solution.py:293
  18.5 0.1 pad_add_fusion.refs_0_.flag_ref
  18.6 0.0 copy-done.15
  18.6 0.0 copy-done.1
  18.6 0.0 copy-done.2
  18.6 0.0 copy-done.3
  18.7 0.0 copy-done.4
  18.7 0.0 copy-start.5
  18.7 1.0 copy-done.5
  19.7 1.0 copy-done.6
  20.6 6.3 %queries.1 = (bf16[4,512,512]{2,1,0:T(8,128)(2,1)}, bf16[320,512]{1,0:T(8,128)(2,1)S(1)}, bf16[384,320]{1,0:T(8,128)(2,1)S(1)}, bf16[384,320]{1,0:T(8,128)(2,1)S(1)}) custom-call(bf16[4,512,320]{2,1,0:T(8,128)(2,1)} %bitcast.10, bf16[1,320]{1,0:T(2,128)(2,1)S(1)} %reshape.21.g_ref.refs_3_.refs_6_.refs_4_, bf16[320,320]{1,0:T(8,128)(2,1)S(1)} %copy-done.1, ...), custom_call_target="tpu_custom_call" | custom-call | flops 3000000000 | bytes 6000000 | tf_op jit(solution)/shard_map/queries/pallas_call | solution.py:64
  26.9 0.0 collective-permute-done.1
  26.9 1.4 %broadcast_select_fusion.1 = bf16[1,512,320]{2,1,0:T(8,128)(2,1)S(1)} fusion(bf16[1,512,320]{2,1,0:T(8,128)(2,1)} %collective-permute-done.1, bf16[1,512,320]{2,1,0:T(8,128)(2,1)} %broadcast_select_fusion, pred[]{:T(512)S(6)} %eq.19), kind=kLoop, calls=%fused_computation.3 | loop fusion | flops 163840 | bytes 983041 | tf_op jit(solution)/shard_map/jit(_where)/select_n | solution.py:295
  28.3 2.1 %collective-permute-start.2 = (bf16[1,512,320]{2,1,0:T(8,128)(2,1)S(1)}, bf16[1,512,320]{2,1,0:T(8,128)(2,1)}, u32[]{:S(2)}, u32[]{:S(2)}) collective-permute-start(bf16[1,512,320]{2,1,0:T(8,128)(2,1)S(1)} %broadcast_select_fusion.1), channel_id=1, source_target_pairs={{0,4},{16,20},{8,12},{24,28},{1,5},{17,21},{9,13},{25,29}} | collective-permute-start | bytes 983048 | tf_op jit(solution)/shard_map/ppermute | solution.py:293
  30.4 0.0 copy-done.9
  30.4 0.0 copy-done.11
  30.4 0.0 copy-done.13
  30.4 0.0 copy-done
  30.4 0.0 copy-start.16
  30.4 0.0 copy-start.17
  30.4 12.0 %own.1 = (f32[4,8,512]{2,1,0:T(8,128)S(1)}, f32[4,384,512]{2,1,0:T(8,128)}) custom-call(s32[4]{0:T(128)S(1)} %pad_add_fusion.refs_0_.flag_ref, bf16[4,512,320]{2,1,0:T(8,128)(2,1)S(1)} %bitcast.14, bf16[4,512,512]{2,1,0:T(8,128)(2,1)} %get-tuple-element.21.refs_2_.refs_5_.refs_3_, bf16[1,320]{1,0:T(2,128)(2,1)S(1)} %reshape.21.g_ref.refs_3_.refs_6_.refs_4_, ...), custom_call_target="tpu_custom_call" | custom-call | flops 8808038400 | bytes 786432 | tf_op jit(solution)/shard_map/own/pallas_call | solution.py:213
  42.4 0.0 copy-done.16
  42.4 0.0 copy-done.17
  42.4 0.0 collective-permute-done.2
  42.4 0.9 broadcast_select_fusion.2
  43.3 1.5 %collective-permute-start.3 = (bf16[1,512,320]{2,1,0:T(8,128)(2,1)}, bf16[1,512,320]{2,1,0:T(8,128)(2,1)S(1)}, u32[]{:S(2)}, u32[]{:S(2)}) collective-permute-start(bf16[1,512,320]{2,1,0:T(8,128)(2,1)} %broadcast_select_fusion.2), channel_id=1, source_target_pairs={{0,2},{16,18},{8,10},{24,26},{4,6},{20,22},{12,14},{28,30},{1,3},{... | collective-permute-start | bytes 983048 | tf_op jit(solution)/shard_map/ppermute | solution.py:293
  44.8 0.0 collective-permute-done.5
  44.8 1.7 %copy.19.refs_1_.refs_4_ = bf16[3,512,320]{2,1,0:T(8,128)(2,1)S(1)} copy(bf16[3,512,320]{1,2,0:T(8,128)(2,1)} %collective-permute-done.5) | data formatting | bytes 1966080 | tf_op jit(solution)/shard_map/ppermute | solution.py:302
  46.4 0.0 copy-done.10
  46.4 0.0 copy-done.12
  46.5 1.6 %copy-done.8 = bf16[4,512,512]{2,1,0:T(8,128)(2,1)S(1)} copy-done((bf16[4,512,512]{2,1,0:T(8,128)(2,1)S(1)}, bf16[4,512,512]{2,1,0:T(8,128)(2,1)}, u32[]{:S(2)}) %copy-start.8) | copy-done | bytes 2097176
  48.1 12.3 %side.1 = (f32[4,8,512]{2,1,0:T(8,128)S(1)}, f32[4,384,512]{2,1,0:T(8,128)}) custom-call(s32[4]{0:T(128)S(1)} %pad_add_fusion.refs_0_.flag_ref, bf16[3,512,320]{2,1,0:T(8,128)(2,1)S(1)} %copy.19.refs_1_.refs_4_, bf16[4,512,512]{2,1,0:T(8,128)(2,1)S(1)} %copy-done.8, ...), custom_call_target="tpu_custom_call", output_to_operand_aliasing={{0}: (6, {}), {1}: (7, {})} | custom-call | flops 8808038400 | bytes 786432 | tf_op jit(solution)/shard_map/side/pallas_call | solution.py:213
  60.4 0.0 collective-permute-done.6.refs_1_
  60.4 0.0 collective-permute-done.7.refs_2_
  60.4 9.0 %prev.1 = (f32[4,8,512]{2,1,0:T(8,128)S(1)}, f32[4,384,512]{2,1,0:T(8,128)}) custom-call(s32[4]{0:T(128)S(1)} %pad_add_fusion.refs_0_.flag_ref, bf16[1,512,320]{2,1,0:T(8,128)(2,1)S(1)} %collective-permute-done.6.refs_1_, bf16[1,512,320]{2,1,0:T(8,128)(2,1)S(1)} %collective-permute-done.7.refs_2_, bf16[4,512,320]{2,1,0:T(8,128)(2,1)} %bitcast.11, ...), custom_call_target="tpu_custom_call" | custom-call | flops 5872025600 | bytes 524288 | tf_op jit(solution)/shard_map/prev/pallas_call | solution.py:213
  69.4 0.0 collective-permute-done.3
  69.4 1.1 broadcast_select_fusion.3.refs_1_
  70.5 1.6 %collective-permute-start.4 = (bf16[1,512,320]{2,1,0:T(8,128)(2,1)S(1)}, bf16[1,512,320]{2,1,0:T(8,128)(2,1)S(1)}, u32[]{:S(2)}, u32[]{:S(2)}) collective-permute-start(bf16[1,512,320]{2,1,0:T(8,128)(2,1)S(1)} %broadcast_select_fusion.3.refs_1_), channel_id=1, source_target_pairs={{0,1},{1,0},{2,3},{3,2},{4,5},{5,4},{6,7},{7,6},{8,9},{9,8},{10,11... | collective-permute-start | bytes 983048 | tf_op jit(solution)/shard_map/ppermute | solution.py:302
  72.0 2.1 %slice_dynamic-update-slice_fusion.refs_8_ = f32[4,384,512]{2,1,0:T(8,128)} fusion(f32[4,384,512]{2,1,0:T(8,128)} %get-tuple-element.28, f32[4,384,512]{2,1,0:T(8,128)} %get-tuple-element.29), kind=kLoop, calls=%fused_computation.1 | loop fusion | bytes 1572864 | tf_op jit(solution)/shard_map/dynamic_update_slice | solution.py:333
  74.1 4.2 %collective-permute-done.4.refs_2_ = bf16[1,512,320]{2,1,0:T(8,128)(2,1)S(1)} collective-permute-done((bf16[1,512,320]{2,1,0:T(8,128)(2,1)S(1)}, bf16[1,512,320]{2,1,0:T(8,128)(2,1)S(1)}, u32[]{:S(2)}, u32[]{:S(2)}) %collective-permute-start.4) | collective-permute-done | bytes 327712 | tf_op jit(solution)/shard_map/ppermute | solution.py:302
  78.3 15.5 %lead.2 = (bf16[2,512,320]{2,1,0:T(8,128)(2,1)S(1)}, f32[2,40,320]{2,1,0:T(8,128)S(1)}, f32[2,8,320]{2,1,0:T(8,128)S(1)}) custom-call(s32[4]{0:T(128)S(1)} %pad_add_fusion.refs_0_.flag_ref, bf16[1,512,320]{2,1,0:T(8,128)(2,1)S(1)} %broadcast_select_fusion.3.refs_1_, bf16[1,512,320]{2,1,0:T(8,128)(2,1)S(1)} %collective-permute-done.4.refs_2_, ...), custom_call_target="tpu_custom_call" | custom-call | flops 11744051200 | bytes 1048576 | tf_op jit(solution)/shard_map/lead/pallas_call | solution.py:213
  93.8 0.0 copy-start.7
  93.9 1.6 %collective-permute-start.8 = (f32[2,40,320]{2,1,0:T(8,128)S(1)}, f32[2,40,320]{2,1,0:T(8,128)S(1)}, u32[]{:S(2)}, u32[]{:S(2)}) collective-permute-start(f32[2,40,320]{2,1,0:T(8,128)S(1)} %get-tuple-element.32), channel_id=1, source_target_pairs={{0,1},{1,0},{2,3},{3,2},{4,5},{5,4},{6,7},{7,6},{8,9},{9,8},{10,11... | collective-permute-start | bytes 307208 | tf_op jit(solution)/shard_map/ppermute | solution.py:341
  95.4 15.5 %lead.3 = (bf16[2,512,320]{2,1,0:T(8,128)(2,1)S(1)}, f32[2,40,320]{2,1,0:T(8,128)S(1)}, f32[2,8,320]{2,1,0:T(8,128)S(1)}) custom-call(s32[4]{0:T(128)S(1)} %pad_add_fusion.refs_0_.flag_ref, bf16[1,512,320]{2,1,0:T(8,128)(2,1)S(1)} %broadcast_select_fusion.3.refs_1_, bf16[1,512,320]{2,1,0:T(8,128)(2,1)S(1)} %collective-permute-done.4.refs_2_, ...), custom_call_target="tpu_custom_call" | custom-call | flops 11744051200 | bytes 1048576 | tf_op jit(solution)/shard_map/lead/pallas_call | solution.py:213
  111.0 0.6 collective-permute-start.9
  111.5 0.0 collective-permute-done.8.top_ref.bot_ref
  111.6 7.3 %conv.2 = bf16[2,512,320]{2,1,0:T(8,128)(2,1)S(1)} custom-call(s32[4]{0:T(128)S(1)} %pad_add_fusion.refs_0_.flag_ref, bf16[2,512,320]{2,1,0:T(8,128)(2,1)S(1)} %get-tuple-element.31.upd_ref, f32[2,40,320]{2,1,0:T(8,128)S(1)} %collective-permute-done.8.top_ref.bot_ref, f32[2,40,320]{2,1,0:T(8,128)S(1)} %collective-permute-done.8.top_ref.bot_ref, ...), custom_call_target="tpu_custom_call" | custom-call | flops 4194304000 | bytes 4000000 | tf_op jit(solution)/shard_map/conv/pallas_call | solution.py:269
  118.9 0.0 collective-permute-done.9.top_ref.bot_ref
  118.9 7.7 %conv.3 = bf16[2,512,320]{2,1,0:T(8,128)(2,1)S(1)} custom-call(s32[4]{0:T(128)S(1)} %pad_add_fusion.refs_0_.flag_ref, bf16[2,512,320]{2,1,0:T(8,128)(2,1)S(1)} %get-tuple-element.34.upd_ref, f32[2,40,320]{2,1,0:T(8,128)S(1)} %collective-permute-done.9.top_ref.bot_ref, f32[2,40,320]{2,1,0:T(8,128)S(1)} %collective-permute-done.9.top_ref.bot_ref, ...), custom_call_target="tpu_custom_call" | custom-call | flops 4194304000 | bytes 4000000 | tf_op jit(solution)/shard_map/conv/pallas_call | solution.py:269
  126.6 1.4 %pad_maximum_fusion = bf16[4,512,320]{2,1,0:T(8,128)(2,1)} fusion(bf16[2,512,320]{2,1,0:T(8,128)(2,1)S(1)} %conv.3, bf16[2,512,320]{2,1,0:T(8,128)(2,1)S(1)} %conv.2), kind=kLoop, calls=%fused_computation | loop fusion | flops 655360 | bytes 2621440 | tf_op jit(solution)/shard_map/concatenate | solution.py:350
  (16 shorter events, 0.0 us)
Async XLA Ops:
  0.0 11.5 %slice-start = ((bf16[4,16,32,320]{3,2,1,0:T(8,128)(2,1)}), bf16[3,16,32,320]{3,2,1,0:T(8,128)(2,1)S(1)}, s32[]{:S(2)}) async-start(bf16[4,16,32,320]{3,2,1,0:T(8,128)(2,1)} %param.12), calls=%async_computation | async-start | bytes 2359296 | tf_op jit(solution)/shard_map/slice | solution.py:320
  2.1 12.3 %collective-permute-start = (bf16[1,512,320]{2,1,0:T(8,128)(2,1)S(1)}, bf16[1,512,320]{2,1,0:T(8,128)(2,1)}, u32[]{:S(2)}, u32[]{:S(2)}) collective-permute-start(bf16[1,512,320]{2,1,0:T(8,128)(2,1)S(1)} %bitcast.16), channel_id=1, source_target_pairs={{0,16},{1,17}} | collective-permute-start | bytes 983048 | tf_op jit(solution)/shard_map/ppermute | solution.py:293
  8.7 51.6 %collective-permute-start.6 = (bf16[1,512,320]{2,1,0:T(8,128)(2,1)}, bf16[1,512,320]{2,1,0:T(8,128)(2,1)S(1)}, u32[]{:S(2)}, u32[]{:S(2)}) collective-permute-start(bf16[1,512,320]{2,1,0:T(8,128)(2,1)} %bitcast.7), channel_id=1, source_target_pairs={{0,2},{1,3},{2,4},{3,5},{4,6},{5,7},{6,8},{7,9},{8,10},{9,11},{10,... | collective-permute-start | bytes 983048 | tf_op jit(solution)/shard_map/ppermute | solution.py:321
  10.1 50.3 %collective-permute-start.7 = (bf16[1,512,320]{2,1,0:T(8,128)(2,1)}, bf16[1,512,320]{2,1,0:T(8,128)(2,1)S(1)}, u32[]{:S(2)}, u32[]{:S(2)}) collective-permute-start(bf16[1,512,320]{2,1,0:T(8,128)(2,1)} %bitcast.7), channel_id=1, source_target_pairs={{0,3},{1,2},{2,5},{3,4},{4,7},{5,6},{6,9},{7,8},{8,11},{9,10},{10,... | collective-permute-start | bytes 983048 | tf_op jit(solution)/shard_map/ppermute | solution.py:321
  11.5 7.1 %copy-start.15 = (bf16[320]{0:T(512)(128)(2,1)S(1)}, bf16[320]{0:T(512)(128)(2,1)}, u32[]{:S(2)}) copy-start(bf16[320]{0:T(512)(128)(2,1)} %param.13) | copy-start | bytes 1924
  11.5 7.1 %copy-start.1 = (bf16[320,320]{1,0:T(8,128)(2,1)S(1)}, bf16[320,320]{1,0:T(8,128)(2,1)}, u32[]{:S(2)}) copy-start(bf16[320,320]{1,0:T(8,128)(2,1)} %wq_ref.1) | copy-start | bytes 614404
  11.5 7.1 %copy-start.2 = (bf16[320,320]{1,0:T(8,128)(2,1)S(1)}, bf16[320,320]{1,0:T(8,128)(2,1)}, u32[]{:S(2)}) copy-start(bf16[320,320]{1,0:T(8,128)(2,1)} %wk_ref.1) | copy-start | bytes 614404
  11.5 7.1 %copy-start.3 = (bf16[320,320]{1,0:T(8,128)(2,1)S(1)}, bf16[320,320]{1,0:T(8,128)(2,1)}, u32[]{:S(2)}) copy-start(bf16[320,320]{1,0:T(8,128)(2,1)} %wv_ref.1) | copy-start | bytes 614404
  11.5 7.1 %copy-start.4 = (bf16[320,320]{1,0:T(8,128)(2,1)S(1)}, bf16[320,320]{1,0:T(8,128)(2,1)}, u32[]{:S(2)}) copy-start(bf16[320,320]{1,0:T(8,128)(2,1)} %wo_ref.1) | copy-start | bytes 614404
  12.9 31.8 %collective-permute-start.5 = (bf16[3,512,320]{1,2,0:T(8,128)(2,1)}, bf16[3,512,320]{1,2,0:T(8,128)(2,1)}, u32[]{:S(2)}, u32[]{:S(2)}) collective-permute-start(bf16[3,512,320]{1,2,0:T(8,128)(2,1)} %copy.18), channel_id=1, source_target_pairs={{0,1},{1,0},{2,3},{3,2},{4,5},{5,4},{6,7},{7,6},{8,9},{9,8},{10,11... | collective-permute-start | bytes 2949128 | tf_op jit(solution)/shard_map/ppermute | solution.py:302
  15.2 11.7 %collective-permute-start.1 = (bf16[1,512,320]{2,1,0:T(8,128)(2,1)}, bf16[1,512,320]{2,1,0:T(8,128)(2,1)}, u32[]{:S(2)}, u32[]{:S(2)}) collective-permute-start(bf16[1,512,320]{2,1,0:T(8,128)(2,1)} %broadcast_select_fusion), channel_id=1, source_target_pairs={{0,8},{16,24},{1,9},{17,25}} | collective-permute-start | bytes 983048 | tf_op jit(solution)/shard_map/ppermute | solution.py:293
  18.7 1.0 copy-start.5
  19.7 1.0 copy-start.6
  20.6 9.7 %copy-start = (bf16[4,16,32,320]{3,2,1,0:T(8,128)(2,1)S(1)}, bf16[4,16,32,320]{3,2,1,0:T(8,128)(2,1)}, u32[]{:S(2)}) copy-start(bf16[4,16,32,320]{3,2,1,0:T(8,128)(2,1)} %param.12) | copy-start | bytes 3932164
  26.9 3.4 %copy-start.9 = (bf16[320,512]{1,0:T(8,128)(2,1)}, bf16[320,512]{1,0:T(8,128)(2,1)S(1)}, u32[]{:S(2)}) copy-start(bf16[320,512]{1,0:T(8,128)(2,1)S(1)} %get-tuple-element.22.refs_4_.refs_7_.refs_5_) | copy-start | bytes 983044
  26.9 3.4 %copy-start.11 = (bf16[384,320]{1,0:T(8,128)(2,1)}, bf16[384,320]{1,0:T(8,128)(2,1)S(1)}, u32[]{:S(2)}) copy-start(bf16[384,320]{1,0:T(8,128)(2,1)S(1)} %get-tuple-element.23.refs_5_.refs_8_.refs_6_) | copy-start | bytes 737284
  26.9 3.4 %copy-start.13 = (bf16[384,320]{1,0:T(8,128)(2,1)}, bf16[384,320]{1,0:T(8,128)(2,1)S(1)}, u32[]{:S(2)}) copy-start(bf16[384,320]{1,0:T(8,128)(2,1)S(1)} %get-tuple-element.30.refs_10_) | copy-start | bytes 737284
  28.3 14.1 %collective-permute-start.2 = (bf16[1,512,320]{2,1,0:T(8,128)(2,1)S(1)}, bf16[1,512,320]{2,1,0:T(8,128)(2,1)}, u32[]{:S(2)}, u32[]{:S(2)}) collective-permute-start(bf16[1,512,320]{2,1,0:T(8,128)(2,1)S(1)} %broadcast_select_fusion.1), channel_id=1, source_target_pairs={{0,4},{16,20},{8,12},{24,28},{1,5},{17,21},{9,13},{25,29}} | collective-permute-start | bytes 983048 | tf_op jit(solution)/shard_map/ppermute | solution.py:293
  30.4 12.0 %copy-start.16 = (bf16[320]{0:T(512)(128)(2,1)S(1)}, bf16[320]{0:T(512)(128)(2,1)}, u32[]{:S(2)}) copy-start(bf16[320]{0:T(512)(128)(2,1)} %param.18) | copy-start | bytes 1924
  30.4 12.0 %copy-start.17 = (bf16[320]{0:T(512)(128)(2,1)S(1)}, bf16[320]{0:T(512)(128)(2,1)}, u32[]{:S(2)}) copy-start(bf16[320]{0:T(512)(128)(2,1)} %param.20) | copy-start | bytes 1924
  42.4 4.1 %copy-start.10 = (bf16[320,512]{1,0:T(8,128)(2,1)S(1)}, bf16[320,512]{1,0:T(8,128)(2,1)}, u32[]{:S(2)}) copy-start(bf16[320,512]{1,0:T(8,128)(2,1)} %copy-done.9) | copy-start | bytes 983044
  42.4 4.1 %copy-start.12 = (bf16[384,320]{1,0:T(8,128)(2,1)S(1)}, bf16[384,320]{1,0:T(8,128)(2,1)}, u32[]{:S(2)}) copy-start(bf16[384,320]{1,0:T(8,128)(2,1)} %copy-done.11) | copy-start | bytes 737284
  43.3 26.1 %collective-permute-start.3 = (bf16[1,512,320]{2,1,0:T(8,128)(2,1)}, bf16[1,512,320]{2,1,0:T(8,128)(2,1)S(1)}, u32[]{:S(2)}, u32[]{:S(2)}) collective-permute-start(bf16[1,512,320]{2,1,0:T(8,128)(2,1)} %broadcast_select_fusion.2), channel_id=1, source_target_pairs={{0,2},{16,18},{8,10},{24,26},{4,6},{20,22},{12,14},{28,30},{1,3},{... | collective-permute-start | bytes 983048 | tf_op jit(solution)/shard_map/ppermute | solution.py:293
  46.5 1.6 %copy-start.8 = (bf16[4,512,512]{2,1,0:T(8,128)(2,1)S(1)}, bf16[4,512,512]{2,1,0:T(8,128)(2,1)}, u32[]{:S(2)}) copy-start(bf16[4,512,512]{2,1,0:T(8,128)(2,1)} %get-tuple-element.21.refs_2_.refs_5_.refs_3_) | copy-start | bytes 6291460
  69.4 9.0 %copy-start.14 = (bf16[384,320]{1,0:T(8,128)(2,1)S(1)}, bf16[384,320]{1,0:T(8,128)(2,1)}, u32[]{:S(2)}) copy-start(bf16[384,320]{1,0:T(8,128)(2,1)} %copy-done.13) | copy-start | bytes 737284
  70.5 7.8 %collective-permute-start.4 = (bf16[1,512,320]{2,1,0:T(8,128)(2,1)S(1)}, bf16[1,512,320]{2,1,0:T(8,128)(2,1)S(1)}, u32[]{:S(2)}, u32[]{:S(2)}) collective-permute-start(bf16[1,512,320]{2,1,0:T(8,128)(2,1)S(1)} %broadcast_select_fusion.3.refs_1_), channel_id=1, source_target_pairs={{0,1},{1,0},{2,3},{3,2},{4,5},{5,4},{6,7},{7,6},{8,9},{9,8},{10,11... | collective-permute-start | bytes 983048 | tf_op jit(solution)/shard_map/ppermute | solution.py:302
  93.8 17.7 %copy-start.7 = (bf16[320,320]{1,0:T(8,128)(2,1)S(1)}, bf16[320,320]{1,0:T(8,128)(2,1)}, u32[]{:S(2)}) copy-start(bf16[320,320]{1,0:T(8,128)(2,1)} %constant.61.clone.group_ref) | copy-start | bytes 614404
  93.9 17.7 %collective-permute-start.8 = (f32[2,40,320]{2,1,0:T(8,128)S(1)}, f32[2,40,320]{2,1,0:T(8,128)S(1)}, u32[]{:S(2)}, u32[]{:S(2)}) collective-permute-start(f32[2,40,320]{2,1,0:T(8,128)S(1)} %get-tuple-element.32), channel_id=1, source_target_pairs={{0,1},{1,0},{2,3},{3,2},{4,5},{5,4},{6,7},{7,6},{8,9},{9,8},{10,11... | collective-permute-start | bytes 307208 | tf_op jit(solution)/shard_map/ppermute | solution.py:341
  111.0 7.9 %collective-permute-start.9 = (f32[2,40,320]{2,1,0:T(8,128)S(1)}, f32[2,40,320]{2,1,0:T(8,128)S(1)}, u32[]{:S(2)}, u32[]{:S(2)}) collective-permute-start(f32[2,40,320]{2,1,0:T(8,128)S(1)} %get-tuple-element.35), channel_id=1, source_target_pairs={{0,1},{1,0},{2,3},{3,2},{4,5},{5,4},{6,7},{7,6},{8,9},{9,8},{10,11... | collective-permute-start | bytes 307208 | tf_op jit(solution)/shard_map/ppermute | solution.py:341

commit v2 on v1

v2 whole, which is shorter than its diff:
```python
import functools
import math

import jax
import jax.numpy as jnp
from jax import lax
from jax.experimental import pallas as pl
from jax.experimental.pallas import tpu as pltpu
from jax.sharding import PartitionSpec as P

HEADS = 8
GROUPS = 32
KPAD = 64
VPAD = 48
BF16, F32, I32 = jnp.bfloat16, jnp.float32, jnp.int32
VMEM_BYTES = 28 * 2**20


def nt(a, b):
    return lax.dot_general(a, b, (((1,), (1,)), ((), ())), preferred_element_type=F32)


def params():
    return pltpu.CompilerParams(vmem_limit_bytes=VMEM_BYTES, dimension_semantics=("arbitrary",))


def cost(flops, moved, exps=0):
    return pl.CostEstimate(flops=int(flops), bytes_accessed=int(moved), transcendentals=int(exps))


def whole(a):
    return pl.BlockSpec(a.shape, lambda i: (0,) * len(a.shape))


def blocked(a, index):
    return pl.BlockSpec((1,) + a.shape[1:], lambda i: (index(i),) + (0,) * (len(a.shape) - 1))


def shape_of(*dims, dtype=BF16):
    return jax.ShapeDtypeStruct(dims, dtype)


def head_spread(channels, pad):
    dim = channels // HEADS
    shape = (HEADS * pad, channels)
    row = lax.broadcasted_iota(I32, shape, 0)
    col = lax.broadcasted_iota(I32, shape, 1)
    head = sum((row >= h * pad).astype(I32) for h in range(1, HEADS))
    inside = row - head * pad
    return jnp.where((inside < dim) & (head * dim + inside == col), 1.0, 0.0).astype(BF16)


def project_kernel(x_ref, g_ref, wq_ref, wk_ref, wv_ref, wo_ref,
                   qt_ref, main_ref, first_ref, last_ref, wkp_ref, wvt_ref, wop_ref, wqt_ref):
    i, n = pl.program_id(0), pl.num_programs(0)
    ch = g_ref.shape[1]

    @pl.when(i == 0)
    def _():
        ek, ev = head_spread(ch, KPAD), head_spread(ch, VPAD)
        wqt_ref[...] = nt(ek, wq_ref[...]).astype(BF16)
        wkp_ref[...] = nt(wk_ref[...], ek).astype(BF16)
        wvt_ref[...] = nt(ev, wv_ref[...]).astype(BF16)
        wop_ref[...] = jnp.dot(ev, wo_ref[...], preferred_element_type=F32).astype(BF16)

    floated = x_ref[0].astype(F32)
    centre = floated - jnp.mean(floated, axis=-1, keepdims=True)
    spread = jnp.mean(centre * centre, axis=-1, keepdims=True)
    normed = (centre * lax.rsqrt(spread + 1e-05) * g_ref[...].astype(F32)).astype(BF16)

    @pl.when(i < n - 1)
    def _():
        main_ref[0] = normed

    @pl.when(i == 0)
    def _():
        first_ref[0] = normed

    @pl.when(i == n - 1)
    def _():
        last_ref[0] = normed

    qt_ref[0] = nt(wqt_ref[...], normed).astype(BF16)


def project(x, gain, wq, wk, wv, wo):
    frames, tok, ch = x.shape
    nk, nv = HEADS * KPAD, HEADS * VPAD
    outs = [shape_of(frames, nk, tok), shape_of(frames - 1, tok, ch), shape_of(1, tok, ch), shape_of(1, tok, ch),
            shape_of(ch, nk), shape_of(nv, ch), shape_of(nv, ch)]
    each = lambda i: i
    return pl.pallas_call(
        project_kernel,
        grid=(frames,),
        in_specs=[blocked(x, each)] + [whole(a) for a in (gain, wq, wk, wv, wo)],
        out_specs=[blocked(outs[0], each), blocked(outs[1], lambda i: jnp.minimum(i, frames - 2))]
        + [whole(o) for o in outs[2:]],
        out_shape=outs,
        scratch_shapes=[pltpu.VMEM((nk, ch), BF16)],
        compiler_params=params(),
        cost_estimate=cost(frames * tok * ch * nk * 8, 8e6),
        name="project",
    )(x, gain, wq, wk, wv, wo)


def flash_kernel(cfg, *refs):
    late, first, last, rows, pair = cfg
    refs = list(refs)
    take = lambda n: [refs.pop(0) for _ in range(n)]
    seg_ref, segn_ref = take(2)
    late_ref = refs.pop(0) if late else None
    qt_ref, qtn_ref, wkp_ref, wvt_ref = take(4)
    if not first:
        m_in, acc_in = take(2)
    if last:
        x_ref, wop_ref, upd_ref, edge_ref, stat_ref = take(5)
    else:
        m_out, acc_out = take(2)
    k_ref, vt_ref, s_ref = take(3)
    if last:
        att_ref = refs.pop(0)
    i, n = pl.program_id(0), pl.num_programs(0)
    tok, ch = qt_ref.shape[2], wkp_ref.shape[0]
    keys = seg_ref.shape[1]
    dim = ch // HEADS
    factor = math.log2(math.e) / math.sqrt(dim)
    once = not late
    zeros = jnp.zeros((KPAD, tok), BF16)
    ones_row = lax.broadcasted_iota(I32, (16, keys), 0) == dim % 16

    def make_keys(seg):
        k_ref[...] = jnp.dot(seg, wkp_ref[...], preferred_element_type=F32).astype(BF16)

    def make_values(seg):
        vt = nt(wvt_ref[...], seg).astype(BF16)
        for h in range(HEADS):
            at = h * VPAD + dim // 16 * 16
            vt_ref[h * VPAD:at] = vt[h * VPAD:at]
            vt_ref[at:at + 16] = jnp.where(ones_row, jnp.ones((16, keys), BF16), vt[at:at + 16])
            if at + 16 < (h + 1) * VPAD:
                vt_ref[at + 16:(h + 1) * VPAD] = vt[at + 16:(h + 1) * VPAD]

    def scores(q_ref, h):
        own = q_ref[0, h * KPAD:(h + 1) * KPAD, :]
        both = jnp.concatenate([own, zeros] if h % 2 == 0 else [zeros, own], axis=0)
        lanes = h // 2 * 2 * KPAD
        s_ref[h % 2] = jnp.dot(k_ref[:, lanes:lanes + 2 * KPAD], both, preferred_element_type=F32)

    @pl.when(i == 0)
    def _():
        seg = seg_ref[0]
        make_keys(seg)
        make_values(seg)
        scores(qt_ref, 0)

    if not once:
        segn = segn_ref[0]
        use_late = (i >= n - 2) & (lax.axis_index("frame") > 0)
        segn = jnp.where(use_late, late_ref[0], segn)

    for h in range(HEADS):
        top = jnp.max(s_ref[h % 2], axis=0, keepdims=True)
        if h + 1 < HEADS:
            scores(qt_ref, h + 1)
        else:
            if not once:
                make_keys(segn)
            scores(qtn_ref, 0)
        if not first:
            old = m_in[0, h:h + 1, :]
            top = jnp.maximum(top, old)
        weights = jnp.exp2((s_ref[h % 2] - top) * factor).astype(BF16)
        part = jnp.dot(vt_ref[h * VPAD:(h + 1) * VPAD, :], weights, preferred_element_type=F32)
        if not first:
            part = part + acc_in[0, h * VPAD:(h + 1) * VPAD, :] * jnp.exp2((old - top) * factor)
        if last:
            att_ref[h * VPAD:(h + 1) * VPAD, :] = (part / part[dim:dim + 1]).astype(BF16)
        else:
            m_out[0, h:h + 1, :] = top
            acc_out[0, h * VPAD:(h + 1) * VPAD, :] = part
    if not once:
        make_values(segn)

    if last:
        mixed = lax.dot_general(att_ref[...], wop_ref[...], (((0,), (0,)), ((), ())),
                                preferred_element_type=F32)
        updated = (x_ref[0].astype(F32) + mixed).astype(BF16)
        upd_ref[0] = updated
        floated = updated.astype(F32)
        cols = tok // rows
        sums = jnp.sum(floated, axis=0, keepdims=True)
        squares = jnp.sum(floated * floated, axis=0, keepdims=True)
        which = lax.broadcasted_iota(I32, (8, ch), 0)
        stats = jnp.where(which == 0, sums, jnp.where(which == 1, squares, 0.0))
        stat_ref[0] = stats
        if pair:
            edge_ref[0, 0:cols] = jnp.where(lax.axis_index("row") == 0, floated[tok - cols:], floated[:cols])
            edge_ref[0, cols:cols + 8] = stats
        else:
            edge_ref[0, 0:cols] = floated[:cols]
            edge_ref[0, cols:2 * cols] = floated[tok - cols:]


def flash(name, frame_of, count, seg, seg_of, qt, wkp, wvt, late=None, state=None, last=None, rows=None, pair=True):
    frames, nk, tok = qt.shape
    ch, nv, keys = wkp.shape[0], wvt.shape[0], seg.shape[1]
    after = lambda i: jnp.minimum(i + 1, count - 1)
    first = state is None
    in_specs = [blocked(seg, seg_of), blocked(seg, lambda i: seg_of(after(i)))]
    args = [seg, seg]
    if late is not None:
        in_specs.append(whole(late))
        args.append(late)
    in_specs += [blocked(qt, frame_of), pl.BlockSpec((1, KPAD, tok), lambda i: (frame_of(after(i)), 0, 0)),
                 whole(wkp), whole(wvt)]
    args += [qt, qt, wkp, wvt]
    state_shapes = [shape_of(frames, HEADS, tok, dtype=F32), shape_of(frames, nv, tok, dtype=F32)]
    state_specs = [blocked(s, frame_of) for s in state_shapes]
    aliases = {}
    scratch = [pltpu.VMEM((keys, nk), BF16), pltpu.VMEM((nv, keys), BF16), pltpu.VMEM((2, keys, tok), F32)]
    if not first:
        if last is None:
            aliases = {len(args): 0, len(args) + 1: 1}
        in_specs += state_specs
        args += list(state)
    if last is None:
        out_shape, out_specs = state_shapes, state_specs
    else:
        x, wop = last
        cols = tok // rows
        in_specs += [blocked(x, frame_of), whole(wop)]
        args += [x, wop]
        out_shape = [shape_of(count, tok, ch), shape_of(count, cols + 8 if pair else 2 * cols, ch, dtype=F32),
                     shape_of(count, 8, ch, dtype=F32)]
        out_specs = [blocked(o, lambda i: i) for o in out_shape]
        scratch.append(pltpu.VMEM((nv, tok), BF16))
    made = count * HEADS * keys * tok
    return pl.pallas_call(
        functools.partial(flash_kernel, (late is not None, first, last is not None, rows, pair)),
        grid=(count,),
        in_specs=in_specs,
        out_specs=out_specs,
        out_shape=out_shape,
        scratch_shapes=scratch,
        input_output_aliases=aliases,
        compiler_params=params(),
        cost_estimate=cost(made * 1400, made // 8, made),
        name=name,
    )(*args)


def conv_kernel(cfg, *refs):
    rows, cols, counted, pair, fresh = cfg
    refs = list(refs)
    take = lambda n: [refs.pop(0) for _ in range(n)]
    upd_ref, top_ref, bot_ref, stat_ref, gn_ref, bias_ref, w_ref = take(7)
    if not fresh:
        refs.pop(0)
    out_ref = refs.pop(0)
    if fresh:
        wide_ref = refs.pop(0)
    (act_ref,) = take(1)
    tok, ch = upd_ref.shape[1:]

    if fresh:
        @pl.when(pl.program_id(0) == 0)
        def _():
            for a in range(3):
                for b in range(3):
                    wide_ref[a * ch:(a + 1) * ch, b * ch:(b + 1) * ch] = w_ref[a, b]
    else:
        wide_ref = w_ref

    stats = stat_ref[0]
    if pair:
        stats = stats + top_ref[0, cols:cols + 8]
    width = ch // GROUPS
    lane = lax.broadcasted_iota(I32, (ch, GROUPS), 0)
    group = lax.broadcasted_iota(I32, (ch, GROUPS), 1)
    member = jnp.where((lane >= group * width) & (lane < (group + 1) * width), 1.0, 0.0)
    exact = functools.partial(lax.dot_general, precision=lax.Precision.HIGHEST, preferred_element_type=F32)
    grouped = exact(stats, member, (((1,), (0,)), ((), ()))) / counted
    mean = grouped[0:1]
    scale = lax.rsqrt(grouped[1:2] - mean * mean + 1e-05)
    which = lax.broadcasted_iota(I32, (8, GROUPS), 0)
    spread = exact(jnp.where(which == 0, mean, jnp.where(which == 1, scale, 0.0)), member, (((1,), (1,)), ((), ())))
    mean, scale = spread[0:1], spread[1:2] * gn_ref[...].astype(F32)

    def activated(u):
        v = (u.astype(F32) - mean) * scale
        return (v / (1.0 + jnp.exp(-v))).astype(BF16)

    me = lax.axis_index("row")
    above = jnp.where(me > 0, activated(top_ref[0, 0:cols]), jnp.zeros((cols, ch), BF16))
    below = jnp.where(me < lax.axis_size("row") - 1, activated(bot_ref[0, 0:cols]), jnp.zeros((cols, ch), BF16))
    middle = activated(upd_ref[0])
    act_ref[:, ch:2 * ch] = middle
    act_ref[0:cols, 0:ch] = above
    act_ref[cols:tok, 0:ch] = middle[0:tok - cols]
    act_ref[0:tok - cols, 2 * ch:] = middle[cols:tok]
    act_ref[tok - cols:tok, 2 * ch:] = below
    parts = jnp.dot(act_ref[...], wide_ref[...], preferred_element_type=F32)
    column = lax.broadcasted_iota(I32, (tok, ch), 0) % cols
    left = jnp.where(column == 0, 0.0, pltpu.roll(parts[:, 0:ch], 1, 0))
    right = jnp.where(column == cols - 1, 0.0, pltpu.roll(parts[:, 2 * ch:], tok - 1, 0))
    total = upd_ref[0].astype(F32) + (left + parts[:, ch:2 * ch] + right) + bias_ref[...].astype(F32)
    out_ref[0] = total.astype(BF16)


def conv(start, frames, upd, top, bot, stats, gn, bias, weight, rows, pair, counted, into=None):
    count, tok, ch = upd.shape
    cols = tok // rows
    each = lambda i: i
    result, wide = shape_of(frames, tok, ch), shape_of(3 * ch, 3 * ch)
    fresh = into is None
    args = [upd, top, bot, stats, gn, bias, weight if fresh else into[1]]
    in_specs = [blocked(a, each) for a in args[:4]] + [whole(a) for a in args[4:]]
    out_shape, out_specs = [result], [blocked(result, lambda i: i + start)]
    if fresh:
        out_shape.append(wide)
        out_specs.append(whole(wide))
    else:
        args.append(into[0])
        in_specs.append(pl.BlockSpec(memory_space=pl.ANY))
    return pl.pallas_call(
        functools.partial(conv_kernel, (rows, cols, counted, pair, fresh)),
        grid=(count,),
        in_specs=in_specs,
        out_specs=out_specs,
        out_shape=out_shape,
        scratch_shapes=[pltpu.VMEM((tok, 3 * ch), BF16)],
        input_output_aliases={} if fresh else {len(args) - 1: 0},
        compiler_params=params(),
        cost_estimate=cost(count * tok * ch * ch * 30, 4e6),
        name="conv",
    )(*args)


def spread_first(value, axis):
    size = lax.axis_size(axis)
    me = lax.axis_index(axis)
    stride = 1
    while stride * 2 < size:
        stride *= 2
    have = [0]
    while stride >= 1:
        new = [i + stride for i in have if i + stride < size]
        if new:
            got = lax.ppermute(value, axis, [(j - stride, j) for j in new])
            value = jnp.where((me & (2 * stride - 1)) == stride, got, value)
            have += new
        stride //= 2
    return value


def others(value, rows):
    got = [lax.ppermute(value, "row", [(i, (i + k) % rows) for i in range(rows)]) for k in range(1, rows)]
    return got[0] if len(got) == 1 else jnp.concatenate(got, axis=1)


def body(latents, ln_gain, q_weight, k_weight, v_weight, o_weight, gn_gain, conv_weight, conv_bias):
    frames, row_count, cols, ch = latents.shape
    tok = row_count * cols
    size, blocks = lax.axis_size("row"), lax.axis_size("frame")
    pair = size == 2
    x = latents.reshape(frames, tok, ch)
    line = lambda v: v.reshape(1, ch)

    qt, main, lead, tail, wkp, wvt, wop = project(x, line(ln_gain), q_weight, k_weight, v_weight, o_weight)
    routes = [[(f * size + r, (f + 1) * size + (r + k) % size) for f in range(blocks - 1) for r in range(size)]
              for k in range(size)]
    came = [lax.ppermute(tail, ("frame", "row"), route) for route in routes]
    prev_side = came[1] if pair else jnp.concatenate(came[1:], axis=1)
    side = others(main, size)
    lead = spread_first(lead, "frame")
    lead_side = others(lead, size)

    common = (qt, wkp, wvt)
    turned = lambda i: lax.rem(i + 1, frames)
    inner = lambda i: lax.rem(i, frames - 1)
    zero = lambda i: 0
    state = flash("own", turned, frames, main, inner, *common, late=came[0])
    state = flash("side", turned, frames, side, inner, *common, late=prev_side, state=state)
    state = flash("lead", lambda i: i, frames, lead, zero, *common, state=state)
    half = frames // 2
    into = None
    finished = []
    for start, count in ((0, half), (half, frames - half)):
        upd, edge, stats = flash("finish", lambda i: i + start, count, lead_side, zero, *common, state=state,
                                 last=(x, wop), rows=row_count, pair=pair)
        if pair:
            top = bot = lax.ppermute(edge, "row", [(0, 1), (1, 0)])
        else:
            top = lax.ppermute(edge[:, cols:], "row", [(i, i + 1) for i in range(size - 1)])
            bot = lax.ppermute(edge[:, :cols], "row", [(i + 1, i) for i in range(size - 1)])
            stats = lax.psum(stats, "row")
        finished.append((start, upd, top, bot, stats))
    for start, upd, top, bot, stats in finished:
        got = conv(start, frames, upd, top, bot, stats, line(gn_gain), line(conv_bias), conv_weight,
                   row_count, pair, tok * size * (ch // GROUPS), into)
        into = (got[0], got[1] if into is None else into[1])
    return into[0].reshape(latents.shape)


def solution(mesh):
    in_specs = (P("frame", "row", None, None), P(), P(), P(), P(), P(), P(), P(), P())
    out_specs = P("frame", "row", None, None)
    return jax.shard_map(body, mesh=mesh, in_specs=in_specs, out_specs=out_specs, check_vma=False)
```

time: 129 us -> 116 us (0.90)
  the two profiles are of different devices: /device:TPU:0 before, /device:TPU:10 now
where the time goes in v2:
time: 116 us; the launch traced here: 115 us
  Pallas kernels  59.7 us (51%)
  starting transfers between devices  26.9 us (23%)
  local copies, waits for them, and re-layouts  20.5 us (18%)
  waiting for transfers between devices  6.21 us (5%)
  other arithmetic  1.96 us (2%)
    pallas_call x5, Pallas kernels, flash(): pl.pallas_call(functools.partial(flash_kernel, (late is not None, first,...  45.3 us
    ppermute x2, starting transfers between devices, body(): came = [lax.ppermute(tail, ('frame', 'row'), route) for route in routes]  17.1 us
    unnamed x36, local copies, waits for them, and re-layouts  16.7 us
    pallas_call x2, Pallas kernels, conv(): pl.pallas_call(functools.partial(conv_kernel, (rows, cols, counted, pair,...  10.2 us
    ppermute x2, waiting for transfers between devices, others(): lax.ppermute(value, 'row', [(i, (i + k) % rows) for i in range(rows)])  6.19 us
    ppermute x4, starting transfers between devices, spread_first(): got = lax.ppermute(value, axis, [(j - stride, j) for j in new])  5.57 us
    pallas_call x1, Pallas kernels, project(): pl.pallas_call(project_kernel, grid=(frames,), in_specs=[blocked(x, each)...  4.19 us
  transfers between devices with their start and end apart: 10, of which 1 were waited for; matrix products, arithmetic and copies ran while one was open for 4% of the time, Pallas kernels for 38%

profile of v2, /device:TPU:10, one launch (start us, length us, event | category | flops | bytes accessed | tf_op | source)
XLA Modules:
  0.0 115.5 jit_solution(12204301005357640657)
XLA Ops:
  0.0 0.7 reshape.18.g_ref
  0.7 0.0 copy-start.1
  0.7 1.4 %copy-done.1 = bf16[4,16,32,320]{3,2,1,0:T(8,128)(2,1)S(1)} copy-done((bf16[4,16,32,320]{3,2,1,0:T(8,128)(2,1)S(1)}, bf16[4,16,32,320]{3,2,1,0:T(8,128)(2,1)}, u32[]{:S(2)}) %copy-start.1) | copy-done | bytes 1310744
  2.1 0.0 copy-start.3
  2.1 0.9 copy-done.3
  3.0 0.0 copy-start.4
  3.0 0.9 copy-done.4
  4.0 0.0 copy-start.5
  4.0 0.9 copy-done.5
  4.9 0.0 copy-start.6
  4.9 0.9 copy-done.6
  5.9 4.2 %project.1 = (bf16[4,512,512]{2,1,0:T(8,128)(2,1)S(1)}, bf16[3,512,320]{2,1,0:T(8,128)(2,1)S(1)}, bf16[1,512,320]{2,1,0:T(8,128)(2,1)S(1)}, bf16[1,512,320]{2,1,...) custom-call(bf16[4,512,320]{2,1,0:T(8,128)(2,1)S(1)} %bitcast.2, ...), custom_call_target="tpu_custom_call" | custom-call | flops 2684354560 | bytes 8000000 | tf_op jit(solution)/shard_map/project/pallas_call | solution.py:92
  10.1 0.0 copy-start.7
  10.1 1.3 %copy-done.7 = bf16[4,512,512]{2,1,0:T(8,128)(2,1)} copy-done((bf16[4,512,512]{2,1,0:T(8,128)(2,1)}, bf16[4,512,512]{2,1,0:T(8,128)(2,1)S(1)}, u32[]{:S(2)}) %copy-start.7) | copy-done | bytes 2097176
  11.4 0.8 collective-permute-start
  12.2 0.0 collective-permute-done
  12.3 0.8 broadcast_select_fusion
  13.0 1.4 %collective-permute-start.1 = (bf16[1,512,320]{2,1,0:T(8,128)(2,1)}, bf16[1,512,320]{2,1,0:T(8,128)(2,1)}, u32[]{:S(2)}, u32[]{:S(2)}) collective-permute-start(bf16[1,512,320]{2,1,0:T(8,128)(2,1)} %broadcast_select_fusion), channel_id=1, source_target_pairs={{0,8},{16,24},{1,9},{17,25}} | collective-permute-start | bytes 983048 | tf_op jit(solution)/shard_map/ppermute | solution.py:349
  14.5 0.0 copy-done.14
  14.5 1.9 %collective-permute-start.7 = (bf16[1,512,320]{2,1,0:T(8,128)(2,1)S(1)}, bf16[1,512,320]{2,1,0:T(8,128)(2,1)S(1)}, u32[]{:S(2)}, u32[]{:S(2)}) collective-permute-start(bf16[1,512,320]{2,1,0:T(8,128)(2,1)S(1)} %get-tuple-element.31), channel_id=1, source_target_pairs={{0,2},{1,3},{2,4},{3,5},{4,6},{5,7},{6,8},{7,9},{8,10},{9,11},{10,... | collective-permute-start | bytes 983048 | tf_op jit(solution)/shard_map/ppermute | solution.py:372
  16.4 15.2 %collective-permute-start.6 = (bf16[1,512,320]{2,1,0:T(8,128)(2,1)S(1)}, bf16[1,512,320]{2,1,0:T(8,128)(2,1)S(1)}, u32[]{:S(2)}, u32[]{:S(2)}) collective-permute-start(bf16[1,512,320]{2,1,0:T(8,128)(2,1)S(1)} %get-tuple-element.31), channel_id=1, source_target_pairs={{0,3},{1,2},{2,5},{3,4},{4,7},{5,6},{6,9},{7,8},{8,11},{9,10},{10,... | collective-permute-start | bytes 983048 | tf_op jit(solution)/shard_map/ppermute | solution.py:372
  31.6 1.4 %copy.15 = bf16[3,512,320]{1,2,0:T(8,128)(2,1)} copy(bf16[3,512,320]{2,1,0:T(8,128)(2,1)S(1)} %get-tuple-element.30.refs_0_.refs_1_) | data formatting | bytes 1966080 | tf_op jit(solution)/shard_map/project/pallas_call | solution.py:92
  32.9 0.5 collective-permute-start.5
  33.5 0.0 copy-done.16
  33.5 0.0 copy-done.17
  33.5 0.0 collective-permute-done.1
  33.5 1.1 broadcast_select_fusion.1
  34.6 1.3 %collective-permute-start.2 = (bf16[1,512,320]{2,1,0:T(8,128)(2,1)S(1)}, bf16[1,512,320]{2,1,0:T(8,128)(2,1)S(1)}, u32[]{:S(2)}, u32[]{:S(2)}) collective-permute-start(bf16[1,512,320]{2,1,0:T(8,128)(2,1)S(1)} %broadcast_select_fusion.1), channel_id=1, source_target_pairs={{0,4},{16,20},{8,12},{24,28},{1,5},{17,21},{9,13},{25,29}} | collective-permute-start | bytes 983048 | tf_op jit(solution)/shard_map/ppermute | solution.py:349
  35.9 0.0 collective-permute-done.7.refs_2_
  35.9 0.0 copy-start.8
  35.9 1.6 %copy-done.8 = bf16[4,512,512]{2,1,0:T(8,128)(2,1)S(1)} copy-done((bf16[4,512,512]{2,1,0:T(8,128)(2,1)S(1)}, bf16[4,512,512]{2,1,0:T(8,128)(2,1)}, u32[]{:S(2)}) %copy-start.8) | copy-done | bytes 2097176
  37.5 11.6 %own.1 = (f32[4,8,512]{2,1,0:T(8,128)S(1)}, f32[4,384,512]{2,1,0:T(8,128)S(1)}) custom-call(bf16[3,512,320]{2,1,0:T(8,128)(2,1)S(1)} %get-tuple-element.30.refs_0_.refs_1_, bf16[3,512,320]{2,1,0:T(8,128)(2,1)S(1)} %get-tuple-element.30.refs_0_.refs_1_, bf16[1,512,320]{2,1,0:T(8,128)(2,1)S(1)} %collective-permute-done.7.refs_2_, ...), custom_call_target="tpu_custom_call" | custom-call | flops 11744051200 | bytes 1048576 | tf_op jit(solution)/shard_map/own/pallas_call | solution.py:238
  49.0 0.0 copy-start.10
  49.1 1.6 %copy-done.10 = f32[4,384,512]{2,1,0:T(8,128)} copy-done((f32[4,384,512]{2,1,0:T(8,128)}, f32[4,384,512]{2,1,0:T(8,128)S(1)}, u32[]{:S(2)}) %copy-start.10) | copy-done | bytes 3145752
  50.7 0.0 collective-permute-done.2
  50.7 2.1 %collective-permute-start.3 = (bf16[1,512,320]{2,1,0:T(8,128)(2,1)S(1)}, bf16[1,512,320]{2,1,0:T(8,128)(2,1)}, u32[]{:S(2)}, u32[]{:S(2)}) collective-permute-start(bf16[1,512,320]{2,1,0:T(8,128)(2,1)S(1)} %broadcast_select_fusion.2), channel_id=1, source_target_pairs={{0,2},{16,18},{8,10},{24,26},{4,6},{20,22},{12,14},{28,30},{1,3},{... | collective-permute-start | bytes 983048 | tf_op jit(solution)/shard_map/ppermute | solution.py:349
  52.8 6.2 %collective-permute-done.5 = bf16[3,512,320]{1,2,0:T(8,128)(2,1)} collective-permute-done((bf16[3,512,320]{1,2,0:T(8,128)(2,1)}, bf16[3,512,320]{1,2,0:T(8,128)(2,1)}, u32[]{:S(2)}, u32[]{:S(2)}) %collective-permute-start.5) | collective-permute-done | bytes 983072 | tf_op jit(solution)/shard_map/ppermute | solution.py:357
  59.0 1.7 %copy.16.refs_0_.refs_1_ = bf16[3,512,320]{2,1,0:T(8,128)(2,1)S(1)} copy(bf16[3,512,320]{1,2,0:T(8,128)(2,1)} %collective-permute-done.5) | data formatting | bytes 1966080 | tf_op jit(solution)/shard_map/ppermute | solution.py:357
  60.6 0.0 collective-permute-done.6.refs_2_
  60.7 0.0 copy-start.9
  60.7 1.6 %copy-done.9 = bf16[4,512,512]{2,1,0:T(8,128)(2,1)S(1)} copy-done((bf16[4,512,512]{2,1,0:T(8,128)(2,1)S(1)}, bf16[4,512,512]{2,1,0:T(8,128)(2,1)}, u32[]{:S(2)}) %copy-start.9) | copy-done | bytes 2097176
  62.3 1.9 %copy-done.11 = f32[4,384,512]{2,1,0:T(8,128)S(1)} copy-done((f32[4,384,512]{2,1,0:T(8,128)S(1)}, f32[4,384,512]{2,1,0:T(8,128)}, u32[]{:S(2)}) %copy-start.11) | copy-done | bytes 3145752
  64.1 11.9 %side.1 = (f32[4,8,512]{2,1,0:T(8,128)S(1)}, f32[4,384,512]{2,1,0:T(8,128)S(1)}) custom-call(bf16[3,512,320]{2,1,0:T(8,128)(2,1)S(1)} %copy.16.refs_0_.refs_1_, bf16[3,512,320]{2,1,0:T(8,128)(2,1)S(1)} %copy.16.refs_0_.refs_1_, bf16[1,512,320]{2,1,0:T(8,128)(2,1)S(1)} %collective-permute-done.6.refs_2_, ...), custom_call_target="tpu_custom_call", output_to_operand_aliasing={{0}: (7, {}), {1}: (8, {})} | custom-call | flops 11744051200 | bytes 1048576 | tf_op jit(solution)/shard_map/side/pallas_call | solution.py:238
  76.0 0.0 collective-permute-done.3
  76.1 0.1 broadcast_select_fusion.3.refs_0_.refs_1_
  76.1 1.6 %collective-permute-start.4 = (bf16[1,512,320]{2,1,0:T(8,128)(2,1)S(1)}, bf16[1,512,320]{2,1,0:T(8,128)(2,1)S(1)}, u32[]{:S(2)}, u32[]{:S(2)}) collective-permute-start(bf16[1,512,320]{2,1,0:T(8,128)(2,1)S(1)} %broadcast_select_fusion.3.refs_0_.refs_1_), channel_id=1, source_target_pairs={{0,1},{1,0},{2,3},{3,2},{4,5},{5,4},{6,7},{7,6},{8,9},{9,8},{10,11... | collective-permute-start | bytes 983048 | tf_op jit(solution)/shard_map/ppermute | solution.py:357
  77.7 9.4 %lead.1 = (f32[4,8,512]{2,1,0:T(8,128)S(1)}, f32[4,384,512]{2,1,0:T(8,128)S(1)}) custom-call(bf16[1,512,320]{2,1,0:T(8,128)(2,1)S(1)} %broadcast_select_fusion.3.refs_0_.refs_1_, bf16[1,512,320]{2,1,0:T(8,128)(2,1)S(1)} %broadcast_select_fusion.3.refs_0_.refs_1_, bf16[4,512,512]{2,1,0:T(8,128)(2,1)S(1)} %copy-done.9, ...), custom_call_target="tpu_custom_call", output_to_operand_aliasing={{0}: (6, {}), {1}: (7, {})} | custom-call | flops 11744051200 | bytes 1048576 | tf_op jit(solution)/shard_map/lead/pallas_call | solution.py:238
  87.1 0.0 copy-start.12
  87.1 1.6 %copy-done.12 = f32[4,384,512]{2,1,0:T(8,128)} copy-done((f32[4,384,512]{2,1,0:T(8,128)}, f32[4,384,512]{2,1,0:T(8,128)S(1)}, u32[]{:S(2)}) %copy-start.12) | copy-done | bytes 3145752
  88.7 0.0 collective-permute-done.4.refs_0_.refs_1_
  88.7 0.0 copy-done.2
  88.7 0.0 copy-done.15
  88.7 0.0 copy-start.13
  88.7 1.9 %copy-done.13 = f32[4,384,512]{2,1,0:T(8,128)S(1)} copy-done((f32[4,384,512]{2,1,0:T(8,128)S(1)}, f32[4,384,512]{2,1,0:T(8,128)}, u32[]{:S(2)}) %copy-start.13) | copy-done | bytes 3145752
  90.6 6.3 %finish.3 = (bf16[2,512,320]{2,1,0:T(8,128)(2,1)S(1)}, f32[2,40,320]{2,1,0:T(8,128)S(1)}, f32[2,8,320]{2,1,0:T(8,128)S(1)}) custom-call(bf16[1,512,320]{2,1,0:T(8,128)(2,1)S(1)} %collective-permute-done.4.refs_0_.refs_1_, bf16[1,512,320]{2,1,0:T(8,128)(2,1)S(1)} %collective-permute-done.4.refs_0_.refs_1_, bf16[4,512,512]{2,1,0:T(8,128)(2,1)S(1)} %copy-done.9, ...), custom_call_target="tpu_custom_call" | custom-call | flops 5872025600 | bytes 524288 | tf_op jit(solution)/shard_map/finish/pallas_call | solution.py:238
  96.9 0.0 copy-start
  96.9 0.6 collective-permute-start.9
  97.5 6.2 %finish.2 = (bf16[2,512,320]{2,1,0:T(8,128)(2,1)S(1)}, f32[2,40,320]{2,1,0:T(8,128)S(1)}, f32[2,8,320]{2,1,0:T(8,128)S(1)}) custom-call(bf16[1,512,320]{2,1,0:T(8,128)(2,1)S(1)} %collective-permute-done.4.refs_0_.refs_1_, bf16[1,512,320]{2,1,0:T(8,128)(2,1)S(1)} %collective-permute-done.4.refs_0_.refs_1_, bf16[4,512,512]{2,1,0:T(8,128)(2,1)S(1)} %copy-done.9, ...), custom_call_target="tpu_custom_call" | custom-call | flops 5872025600 | bytes 524288 | tf_op jit(solution)/shard_map/finish/pallas_call | solution.py:238
  103.7 1.6 %collective-permute-start.8 = (f32[2,40,320]{2,1,0:T(8,128)S(1)}, f32[2,40,320]{2,1,0:T(8,128)S(1)}, u32[]{:S(2)}, u32[]{:S(2)}) collective-permute-start(f32[2,40,320]{2,1,0:T(8,128)S(1)} %get-tuple-element.40), channel_id=1, source_target_pairs={{0,1},{1,0},{2,3},{3,2},{4,5},{5,4},{6,7},{7,6},{8,9},{9,8},{10,11... | collective-permute-start | bytes 307208 | tf_op jit(solution)/shard_map/ppermute | solution.py:392
  105.3 0.0 collective-permute-done.9.refs_1_.refs_2_
  105.3 0.0 copy-done
  105.3 5.3 %conv.2 = (bf16[4,512,320]{2,1,0:T(8,128)(2,1)}, bf16[960,960]{1,0:T(8,128)(2,1)S(1)}) custom-call(bf16[2,512,320]{2,1,0:T(8,128)(2,1)S(1)} %get-tuple-element.42.refs_0_, f32[2,40,320]{2,1,0:T(8,128)S(1)} %collective-permute-done.9.refs_1_.refs_2_, f32[2,40,320]{2,1,0:T(8,128)S(1)} %collective-permute-done.9.refs_1_.refs_2_, ...), custom_call_target="tpu_custom_call" | custom-call | flops 3145728000 | bytes 4000000 | tf_op jit(solution)/shard_map/conv/pallas_call | solution.py:325
  110.6 0.0 collective-permute-done.8.refs_1_.refs_2_
  110.6 4.9 %conv.3 = bf16[4,512,320]{2,1,0:T(8,128)(2,1)} custom-call(bf16[2,512,320]{2,1,0:T(8,128)(2,1)S(1)} %get-tuple-element.39.refs_0_, f32[2,40,320]{2,1,0:T(8,128)S(1)} %collective-permute-done.8.refs_1_.refs_2_, f32[2,40,320]{2,1,0:T(8,128)S(1)} %collective-permute-done.8.refs_1_.refs_2_, ...), custom_call_target="tpu_custom_call", output_to_operand_aliasing={{}: (7, {})} | custom-call | flops 3145728000 | bytes 4000000 | tf_op jit(solution)/shard_map/conv/pallas_call | solution.py:325
  (9 shorter events, 0.1 us)
Async XLA Ops:
  0.7 1.4 %copy-start.1 = (bf16[4,16,32,320]{3,2,1,0:T(8,128)(2,1)S(1)}, bf16[4,16,32,320]{3,2,1,0:T(8,128)(2,1)}, u32[]{:S(2)}) copy-start(bf16[4,16,32,320]{3,2,1,0:T(8,128)(2,1)} %param.9) | copy-start | bytes 3932164
  2.1 0.9 copy-start.3
  3.0 0.9 copy-start.4
  4.0 0.9 copy-start.5
  4.9 0.9 copy-start.6
  10.1 1.4 %copy-start.7 = (bf16[4,512,512]{2,1,0:T(8,128)(2,1)}, bf16[4,512,512]{2,1,0:T(8,128)(2,1)S(1)}, u32[]{:S(2)}) copy-start(bf16[4,512,512]{2,1,0:T(8,128)(2,1)S(1)} %get-tuple-element.27.refs_3_.refs_4_.refs_2_) | copy-start | bytes 6291460
  11.4 3.0 %copy-start.14 = (bf16[384,320]{1,0:T(8,128)(2,1)}, bf16[384,320]{1,0:T(8,128)(2,1)S(1)}, u32[]{:S(2)}) copy-start(bf16[384,320]{1,0:T(8,128)(2,1)S(1)} %get-tuple-element.38.refs_9_) | copy-start | bytes 737284
  11.4 22.0 %copy-start.16 = (bf16[320]{0:T(512)(128)(2,1)S(1)}, bf16[320]{0:T(512)(128)(2,1)}, u32[]{:S(2)}) copy-start(bf16[320]{0:T(512)(128)(2,1)} %param.15) | copy-start | bytes 1924
  11.4 22.0 %copy-start.17 = (bf16[320]{0:T(512)(128)(2,1)S(1)}, bf16[320]{0:T(512)(128)(2,1)}, u32[]{:S(2)}) copy-start(bf16[320]{0:T(512)(128)(2,1)} %param.17) | copy-start | bytes 1924
  11.4 0.8 collective-permute-start
  13.0 20.4 %collective-permute-start.1 = (bf16[1,512,320]{2,1,0:T(8,128)(2,1)}, bf16[1,512,320]{2,1,0:T(8,128)(2,1)}, u32[]{:S(2)}, u32[]{:S(2)}) collective-permute-start(bf16[1,512,320]{2,1,0:T(8,128)(2,1)} %broadcast_select_fusion), channel_id=1, source_target_pairs={{0,8},{16,24},{1,9},{17,25}} | collective-permute-start | bytes 983048 | tf_op jit(solution)/shard_map/ppermute | solution.py:349
  14.5 21.4 %collective-permute-start.7 = (bf16[1,512,320]{2,1,0:T(8,128)(2,1)S(1)}, bf16[1,512,320]{2,1,0:T(8,128)(2,1)S(1)}, u32[]{:S(2)}, u32[]{:S(2)}) collective-permute-start(bf16[1,512,320]{2,1,0:T(8,128)(2,1)S(1)} %get-tuple-element.31), channel_id=1, source_target_pairs={{0,2},{1,3},{2,4},{3,5},{4,6},{5,7},{6,8},{7,9},{8,10},{9,11},{10,... | collective-permute-start | bytes 983048 | tf_op jit(solution)/shard_map/ppermute | solution.py:372
  16.4 44.3 %collective-permute-start.6 = (bf16[1,512,320]{2,1,0:T(8,128)(2,1)S(1)}, bf16[1,512,320]{2,1,0:T(8,128)(2,1)S(1)}, u32[]{:S(2)}, u32[]{:S(2)}) collective-permute-start(bf16[1,512,320]{2,1,0:T(8,128)(2,1)S(1)} %get-tuple-element.31), channel_id=1, source_target_pairs={{0,3},{1,2},{2,5},{3,4},{4,7},{5,6},{6,9},{7,8},{8,11},{9,10},{10,... | collective-permute-start | bytes 983048 | tf_op jit(solution)/shard_map/ppermute | solution.py:372
  32.9 26.0 %collective-permute-start.5 = (bf16[3,512,320]{1,2,0:T(8,128)(2,1)}, bf16[3,512,320]{1,2,0:T(8,128)(2,1)}, u32[]{:S(2)}, u32[]{:S(2)}) collective-permute-start(bf16[3,512,320]{1,2,0:T(8,128)(2,1)} %copy.15), channel_id=1, source_target_pairs={{0,1},{1,0},{2,3},{3,2},{4,5},{5,4},{6,7},{7,6},{8,9},{9,8},{10,11... | collective-permute-start | bytes 2949128 | tf_op jit(solution)/shard_map/ppermute | solution.py:357
  34.6 16.1 %collective-permute-start.2 = (bf16[1,512,320]{2,1,0:T(8,128)(2,1)S(1)}, bf16[1,512,320]{2,1,0:T(8,128)(2,1)S(1)}, u32[]{:S(2)}, u32[]{:S(2)}) collective-permute-start(bf16[1,512,320]{2,1,0:T(8,128)(2,1)S(1)} %broadcast_select_fusion.1), channel_id=1, source_target_pairs={{0,4},{16,20},{8,12},{24,28},{1,5},{17,21},{9,13},{25,29}} | collective-permute-start | bytes 983048 | tf_op jit(solution)/shard_map/ppermute | solution.py:349
  35.9 1.6 %copy-start.8 = (bf16[4,512,512]{2,1,0:T(8,128)(2,1)S(1)}, bf16[4,512,512]{2,1,0:T(8,128)(2,1)}, u32[]{:S(2)}) copy-start(bf16[4,512,512]{2,1,0:T(8,128)(2,1)} %copy-done.7) | copy-start | bytes 6291460
  49.0 1.6 %copy-start.10 = (f32[4,384,512]{2,1,0:T(8,128)}, f32[4,384,512]{2,1,0:T(8,128)S(1)}, u32[]{:S(2)}) copy-start(f32[4,384,512]{2,1,0:T(8,128)S(1)} %get-tuple-element.33.refs_8_) | copy-start | bytes 9437188
  50.7 25.3 %collective-permute-start.3 = (bf16[1,512,320]{2,1,0:T(8,128)(2,1)S(1)}, bf16[1,512,320]{2,1,0:T(8,128)(2,1)}, u32[]{:S(2)}, u32[]{:S(2)}) collective-permute-start(bf16[1,512,320]{2,1,0:T(8,128)(2,1)S(1)} %broadcast_select_fusion.2), channel_id=1, source_target_pairs={{0,2},{16,18},{8,10},{24,26},{4,6},{20,22},{12,14},{28,30},{1,3},{... | collective-permute-start | bytes 983048 | tf_op jit(solution)/shard_map/ppermute | solution.py:349
  60.7 1.6 %copy-start.9 = (bf16[4,512,512]{2,1,0:T(8,128)(2,1)S(1)}, bf16[4,512,512]{2,1,0:T(8,128)(2,1)}, u32[]{:S(2)}) copy-start(bf16[4,512,512]{2,1,0:T(8,128)(2,1)} %copy-done.7) | copy-start | bytes 6291460
  62.2 1.9 %copy-start.11 = (f32[4,384,512]{2,1,0:T(8,128)S(1)}, f32[4,384,512]{2,1,0:T(8,128)}, u32[]{:S(2)}) copy-start(f32[4,384,512]{2,1,0:T(8,128)} %copy-done.10) | copy-start | bytes 9437188
  76.1 12.6 %collective-permute-start.4 = (bf16[1,512,320]{2,1,0:T(8,128)(2,1)S(1)}, bf16[1,512,320]{2,1,0:T(8,128)(2,1)S(1)}, u32[]{:S(2)}, u32[]{:S(2)}) collective-permute-start(bf16[1,512,320]{2,1,0:T(8,128)(2,1)S(1)} %broadcast_select_fusion.3.refs_0_.refs_1_), channel_id=1, source_target_pairs={{0,1},{1,0},{2,3},{3,2},{4,5},{5,4},{6,7},{7,6},{8,9},{9,8},{10,11... | collective-permute-start | bytes 983048 | tf_op jit(solution)/shard_map/ppermute | solution.py:357
  77.7 11.0 %copy-start.2 = (bf16[4,16,32,320]{3,2,1,0:T(8,128)(2,1)S(1)}, bf16[4,16,32,320]{3,2,1,0:T(8,128)(2,1)}, u32[]{:S(2)}) copy-start(bf16[4,16,32,320]{3,2,1,0:T(8,128)(2,1)} %param.9) | copy-start | bytes 3932164
  77.7 11.0 %copy-start.15 = (bf16[384,320]{1,0:T(8,128)(2,1)S(1)}, bf16[384,320]{1,0:T(8,128)(2,1)}, u32[]{:S(2)}) copy-start(bf16[384,320]{1,0:T(8,128)(2,1)} %copy-done.14) | copy-start | bytes 737284
  87.1 1.6 %copy-start.12 = (f32[4,384,512]{2,1,0:T(8,128)}, f32[4,384,512]{2,1,0:T(8,128)S(1)}, u32[]{:S(2)}) copy-start(f32[4,384,512]{2,1,0:T(8,128)S(1)} %get-tuple-element.37.refs_7_) | copy-start | bytes 9437188
  88.7 1.9 %copy-start.13 = (f32[4,384,512]{2,1,0:T(8,128)S(1)}, f32[4,384,512]{2,1,0:T(8,128)}, u32[]{:S(2)}) copy-start(f32[4,384,512]{2,1,0:T(8,128)} %copy-done.12) | copy-start | bytes 9437188
  96.9 8.4 %copy-start = (bf16[3,3,320,320]{3,2,1,0:T(8,128)(2,1)S(1)}, bf16[3,3,320,320]{3,2,1,0:T(8,128)(2,1)}, u32[]{:S(2)}) copy-start(bf16[3,3,320,320]{3,2,1,0:T(8,128)(2,1)} %refs_6_.1) | copy-start | bytes 5529604
  96.9 8.4 %collective-permute-start.9 = (f32[2,40,320]{2,1,0:T(8,128)S(1)}, f32[2,40,320]{2,1,0:T(8,128)S(1)}, u32[]{:S(2)}, u32[]{:S(2)}) collective-permute-start(f32[2,40,320]{2,1,0:T(8,128)S(1)} %get-tuple-element.43), channel_id=1, source_target_pairs={{0,1},{1,0},{2,3},{3,2},{4,5},{5,4},{6,7},{7,6},{8,9},{9,8},{10,11... | collective-permute-start | bytes 307208 | tf_op jit(solution)/shard_map/ppermute | solution.py:392
  103.7 6.9 %collective-permute-start.8 = (f32[2,40,320]{2,1,0:T(8,128)S(1)}, f32[2,40,320]{2,1,0:T(8,128)S(1)}, u32[]{:S(2)}, u32[]{:S(2)}) collective-permute-start(f32[2,40,320]{2,1,0:T(8,128)S(1)} %get-tuple-element.40), channel_id=1, source_target_pairs={{0,1},{1,0},{2,3},{3,2},{4,5},{5,4},{6,7},{7,6},{8,9},{9,8},{10,11... | collective-permute-start | bytes 307208 | tf_op jit(solution)/shard_map/ppermute | solution.py:392

commit v3 on v0

v3 whole, which is shorter than its diff:
```python
import functools
import math

import jax
import jax.numpy as jnp
from jax import lax
from jax.experimental import pallas as pl
from jax.experimental.pallas import tpu as pltpu
from jax.sharding import PartitionSpec as P

HEADS = 8
GROUPS = 32
KPAD = 64
VPAD = 48
BF16, F32, I32 = jnp.bfloat16, jnp.float32, jnp.int32
VMEM_BYTES = 24 * 2**20
LOW = -1e30


def dot(a, b):
    return jnp.dot(a, b, preferred_element_type=F32)


def nt(a, b):
    return lax.dot_general(a, b, (((1,), (1,)), ((), ())), preferred_element_type=F32)


def tn(a, b):
    return lax.dot_general(a, b, (((0,), (0,)), ((), ())), preferred_element_type=F32)


def cost(flops, moved, exps=0):
    return pl.CostEstimate(flops=int(flops), bytes_accessed=int(moved), transcendentals=int(exps))


def near_of(*dims, dtype=BF16):
    return pltpu.VMEM(dims, dtype)


def far_of(*dims, dtype=BF16):
    return pltpu.HBM(dims, dtype)


def near(a):
    return pltpu.with_memory_space_constraint(a, pltpu.VMEM)


def far(a):
    return pltpu.with_memory_space_constraint(a, pltpu.HBM)


def kernel_call(body, name, near_args, far_args, outs, scratch, price, aliases=None):
    in_vmem, anywhere = pl.BlockSpec(memory_space=pltpu.VMEM), pl.BlockSpec(memory_space=pl.ANY)
    return pl.pallas_call(
        body,
        in_specs=[in_vmem] * len(near_args) + [anywhere] * len(far_args),
        out_specs=[in_vmem if o.memory_space == pltpu.VMEM else anywhere for o in outs],
        out_shape=outs,
        scratch_shapes=scratch,
        input_output_aliases=aliases or {},
        compiler_params=pltpu.CompilerParams(vmem_limit_bytes=VMEM_BYTES),
        cost_estimate=price,
        name=name,
    )(*[near(a) for a in near_args], *[far(a) for a in far_args])


def head_spread(channels, pad):
    dim = channels // HEADS
    shape = (HEADS * pad, channels)
    row = lax.broadcasted_iota(I32, shape, 0)
    col = lax.broadcasted_iota(I32, shape, 1)
    head = sum((row >= h * pad).astype(I32) for h in range(1, HEADS))
    inside = row - head * pad
    return jnp.where((inside < dim) & (head * dim + inside == col), 1.0, 0.0).astype(BF16)


def project_kernel(x_hbm, g_hbm, wq_hbm, wk_hbm, wv_hbm, wo_hbm,
                   qt_ref, main_ref, first_ref, last_ref, wkp_ref, wvt_ref, wop_ref,
                   x_ref, g_ref, w_ref, x_sem, w_sem):
    frames, tok, ch = x_ref.shape
    copies = [pltpu.make_async_copy(g_hbm, g_ref, w_sem.at[4])]
    copies += [pltpu.make_async_copy(x_hbm.at[f], x_ref.at[f], x_sem.at[f]) for f in range(frames)]
    weights = [pltpu.make_async_copy(w, w_ref.at[k], w_sem.at[k])
               for k, w in enumerate((wq_hbm, wk_hbm, wv_hbm, wo_hbm))]
    for copy in copies + weights:
        copy.start()
    ek, ev = head_spread(ch, KPAD), head_spread(ch, VPAD)
    copies[0].wait()
    gain = jnp.broadcast_to(g_ref[...].astype(F32).reshape(1, ch), (8, ch)).T[:, 0:1]

    def normed(f):
        copies[1 + f].wait()
        floated = x_ref[f].astype(F32).T
        centre = floated - jnp.sum(floated, axis=0, keepdims=True) / ch
        spread = jnp.sum(centre * centre, axis=0, keepdims=True) / ch
        return (centre * lax.rsqrt(spread + 1e-05) * gain).astype(BF16)

    for f in range(frames):
        value = normed(f)
        if f < frames - 1:
            main_ref[f] = value
        else:
            last_ref[0] = value
        if f == 0:
            first_ref[0] = value
            for copy in weights:
                copy.wait()
            wqt = nt(ek, w_ref[0]).astype(BF16)
            wkp_ref[...] = nt(w_ref[1], ek).astype(BF16)
            wvt_ref[...] = nt(ev, w_ref[2]).astype(BF16)
            wop_ref[...] = dot(ev, w_ref[3]).astype(BF16)
        qt_ref[f] = dot(wqt, value).astype(BF16)


def project(x, gain, wq, wk, wv, wo):
    frames, tok, ch = x.shape
    nk, nv = HEADS * KPAD, HEADS * VPAD
    outs = [near_of(frames, nk, tok), near_of(frames - 1, ch, tok), near_of(1, ch, tok), near_of(1, ch, tok),
            near_of(ch, nk), near_of(nv, ch), near_of(nv, ch)]
    scratch = [pltpu.VMEM(x.shape, BF16), pltpu.VMEM((ch,), BF16), pltpu.VMEM((4, ch, ch), BF16),
               pltpu.SemaphoreType.DMA((frames,)), pltpu.SemaphoreType.DMA((5,))]
    return kernel_call(project_kernel, "project", [], [x, gain, wq, wk, wv, wo], outs, scratch,
                       cost(frames * tok * ch * nk, 8e5))


class Flash:
    def __init__(self, qt_ref, wkp_ref, wvt_ref, state_in, state_out, scratch):
        self.qt, self.wkp, self.wvt = qt_ref, wkp_ref, wvt_ref
        self.state_in, self.state_out = state_in, state_out
        self.acc, self.s, self.in_sem, self.out_sem, *kept = scratch
        if kept:
            self.k, self.vt = kept
        self.tok = qt_ref.shape[2]
        self.dim = wkp_ref.shape[0] // HEADS
        self.factor = math.log2(math.e) / math.sqrt(self.dim)

    def in_copy(self, f):
        return pltpu.make_async_copy(self.state_in.at[f], self.acc.at[f], self.in_sem.at[f])

    def out_copy(self, f):
        return pltpu.make_async_copy(self.acc.at[f], self.state_out.at[f], self.out_sem.at[f])

    def make_keys(self, seg):
        self.k[0:seg.shape[1], :] = tn(seg, self.wkp[...]).astype(BF16)

    def make_values(self, seg):
        keys = seg.shape[1]
        ones_row = lax.broadcasted_iota(I32, (16, keys), 0) == self.dim % 16
        vt = dot(self.wvt[...], seg).astype(BF16)
        for h in range(HEADS):
            at, end = h * VPAD + self.dim // 16 * 16, (h + 1) * VPAD
            self.vt[h * VPAD:at, 0:keys] = vt[h * VPAD:at]
            self.vt[at:at + 16, 0:keys] = jnp.where(ones_row, jnp.ones((16, keys), BF16), vt[at:at + 16])
            if at + 16 < end:
                self.vt[at + 16:end, 0:keys] = vt[at + 16:end]

    def scores(self, f, h, keys):
        own = self.qt[f, h * KPAD:(h + 1) * KPAD, :]
        zeros = jnp.zeros((KPAD, self.tok), BF16)
        both = jnp.concatenate([own, zeros] if h % 2 == 0 else [zeros, own], axis=0)
        lanes = h // 2 * 2 * KPAD
        self.s[h % 2, 0:keys] = dot(self.k[0:keys, lanes:lanes + 2 * KPAD], both)

    def begin(self, f, seg):
        self.make_keys(seg)
        self.make_values(seg)
        self.scores(f, 0, seg.shape[1])

    def item(self, f, keys, after=None, seg=None, first=False, attended=None):
        for h in range(HEADS):
            top = jnp.max(self.s[h % 2, 0:keys], axis=0, keepdims=True)
            if h + 1 < HEADS:
                self.scores(f, h + 1, keys)
            elif after is not None:
                if seg is not None:
                    self.make_keys(seg)
                self.scores(after, 0, keys if seg is None else seg.shape[1])
            rows = slice(h * VPAD, (h + 1) * VPAD)
            if not first:
                kept = self.acc[f, rows, :]
                old = kept[self.dim + 1:self.dim + 2]
                top = jnp.maximum(top, old)
            weights = jnp.exp2((self.s[h % 2, 0:keys] - top) * self.factor).astype(BF16)
            part = dot(self.vt[rows, 0:keys], weights)
            if not first:
                part = part + kept * jnp.exp2((old - top) * self.factor)
            if attended is not None:
                attended[rows, :] = (part / part[self.dim:self.dim + 1]).astype(BF16)
            else:
                self.acc[f, rows, :] = part
                self.acc[f, h * VPAD + self.dim + 1:h * VPAD + self.dim + 2, :] = top
        if after is not None and seg is not None:
            self.make_values(seg)


def own_kernel(qt_ref, wkp_ref, wvt_ref, main_ref, state_out, *scratch):
    flash = Flash(qt_ref, wkp_ref, wvt_ref, None, state_out, scratch)
    frames, keys = qt_ref.shape[0], main_ref.shape[2]
    flash.begin(1, main_ref[0])

    @pl.loop(1, frames - 1)
    def _(f):
        flash.item(f, keys, f + 1, main_ref[f], first=True)
        flash.out_copy(f).start()

    flash.item(frames - 1, keys, first=True)
    flash.out_copy(frames - 1).start()
    for f in range(1, frames):
        flash.out_copy(f).wait()


def side_kernel(qt_ref, wkp_ref, wvt_ref, prev_ref, main_ref, side_ref, state_in, state_out, *scratch):
    flash = Flash(qt_ref, wkp_ref, wvt_ref, state_in, state_out, scratch)
    frames, keys = qt_ref.shape[0], side_ref.shape[2]
    for f in range(1, frames):
        flash.in_copy(f).start()
    flash.begin(0, jnp.where(lax.axis_index("frame") > 0, prev_ref[0], main_ref[0]))
    flash.item(0, prev_ref.shape[2], 1, side_ref[0], first=True)
    flash.out_copy(0).start()

    @pl.loop(1, frames - 1)
    def _(f):
        flash.in_copy(f).wait()
        flash.item(f, keys, f + 1, side_ref[f])
        flash.out_copy(f).start()

    flash.in_copy(frames - 1).wait()
    flash.item(frames - 1, keys)
    flash.out_copy(frames - 1).start()
    for f in range(frames):
        flash.out_copy(f).wait()


def lead_kernel(qt_ref, wkp_ref, wvt_ref, prev_ref, side_ref, lead_ref, state_in, state_out, *scratch):
    flash = Flash(qt_ref, wkp_ref, wvt_ref, state_in, state_out, scratch)
    frames, keys = qt_ref.shape[0], lead_ref.shape[2]
    for f in range(frames):
        flash.in_copy(f).start()
    flash.begin(0, jnp.where(lax.axis_index("frame") > 0, prev_ref[0], side_ref[0]))
    flash.in_copy(0).wait()
    flash.item(0, prev_ref.shape[2], 0, lead_ref[0])
    flash.item(0, keys, 1)
    flash.out_copy(0).start()

    @pl.loop(1, frames - 1)
    def _(f):
        flash.in_copy(f).wait()
        flash.item(f, keys, f + 1)
        flash.out_copy(f).start()

    flash.in_copy(frames - 1).wait()
    flash.item(frames - 1, keys)
    flash.out_copy(frames - 1).start()
    for f in range(frames):
        flash.out_copy(f).wait()


def finish_kernel(start, rows, pair, fresh, *refs):
    refs = list(refs)
    take = lambda n: [refs.pop(0) for _ in range(n)]
    qt_ref, wkp_ref, wvt_ref, wop_ref = take(4)
    if fresh:
        (seg_ref,) = take(1)
    else:
        k_ref, vt_ref = take(2)
    state_hbm, x_hbm, upd_ref, edge_ref, stat_ref = take(5)
    if fresh:
        k_ref, vt_ref = take(2)
    att_ref, x_ref, x_sem = take(3)
    count, tok, ch = x_ref.shape
    cols, keys = tok // rows, k_ref.shape[0]
    flash = Flash(qt_ref, wkp_ref, wvt_ref, state_hbm, None, refs)
    flash.k, flash.vt = k_ref, vt_ref
    for f in range(start, start + count):
        flash.in_copy(f).start()
    copy = pltpu.make_async_copy(x_hbm.at[pl.ds(start, count)], x_ref, x_sem)
    copy.start()
    if fresh:
        flash.begin(start, seg_ref[0])
    else:
        flash.scores(start, 0, keys)

    @pl.loop(0, count)
    def _(i):
        flash.in_copy(start + i).wait()
        flash.item(start + i, keys, start + jnp.minimum(i + 1, count - 1), attended=att_ref)

        @pl.when(i == 0)
        def _():
            copy.wait()

        mixed = tn(att_ref[...], wop_ref[...])
        updated = (x_ref[i].astype(F32) + mixed).astype(BF16)
        upd_ref[i] = updated
        floated = updated.astype(F32)
        sums = jnp.sum(floated, axis=0, keepdims=True)
        squares = jnp.sum(floated * floated, axis=0, keepdims=True)
        which = lax.broadcasted_iota(I32, (8, ch), 0)
        stats = jnp.where(which == 0, sums, jnp.where(which == 1, squares, 0.0))
        stat_ref[i] = stats
        if pair:
            edge_ref[i, 0:cols] = jnp.where(lax.axis_index("row") == 0, floated[tok - cols:], floated[:cols])
            edge_ref[i, cols:cols + 8] = stats
        else:
            edge_ref[i, 0:cols] = floated[:cols]
            edge_ref[i, cols:2 * cols] = floated[tok - cols:]


def flash_scratch(qt, keys, held=True):
    frames, nk, tok = qt.shape
    nv = HEADS * VPAD
    out = [pltpu.VMEM((frames, nv, tok), F32), pltpu.VMEM((2, keys, tok), F32)]
    out += [pltpu.SemaphoreType.DMA((frames,))] * 2
    return out + ([pltpu.VMEM((keys, nk), BF16), pltpu.VMEM((nv, keys), BF16)] if held else [])


def flash_cost(items, keys, tok):
    made = items * HEADS * keys * tok
    return cost(made * 140, made // 80, made // 10)


def flash(body, name, qt, wkp, wvt, segments, state, items):
    frames, _, tok = qt.shape
    keys = max(s.shape[2] for s in segments)
    near_args, far_args = [qt, wkp, wvt] + segments, []
    aliases = {}
    if state is not None:
        far_args.append(state)
        aliases = {len(near_args): 0}
    outs = [far_of(frames, HEADS * VPAD, tok, dtype=F32)]
    return kernel_call(body, name, near_args, far_args, outs, flash_scratch(qt, keys),
                       flash_cost(items, keys, tok), aliases)[0]


def finish(start, count, qt, wkp, wvt, wop, state, lead_side, made, x, rows, pair):
    tok, ch = x.shape[1:]
    cols, nk, nv, keys = tok // rows, HEADS * KPAD, HEADS * VPAD, lead_side.shape[2]
    fresh = made is None
    outs = [near_of(count, tok, ch), near_of(count, cols + 8 if pair else 2 * cols, ch, dtype=F32),
            near_of(count, 8, ch, dtype=F32)]
    if fresh:
        outs += [near_of(keys, nk), near_of(nv, keys)]
    scratch = [pltpu.VMEM((nv, tok), BF16), pltpu.VMEM((count, tok, ch), BF16), pltpu.SemaphoreType.DMA]
    got = kernel_call(functools.partial(finish_kernel, start, rows, pair, fresh), "finish",
                      [qt, wkp, wvt, wop] + ([lead_side] if fresh else list(made)), [state, x], outs,
                      scratch + flash_scratch(qt, keys, held=False), flash_cost(count, keys, tok))
    return got[:3], (tuple(got[3:]) if fresh else made)


def conv_kernel(start, rows, counted, pair, fresh, *refs):
    refs = list(refs)
    take = lambda n: [refs.pop(0) for _ in range(n)]
    upd_ref, top_ref, bot_ref, stat_ref, gn_ref, bias_ref, w_ref = take(7)
    if not fresh:
        take(1)
    (out_hbm,) = take(1)
    if fresh:
        (wide_ref,) = take(1)
    act_ref, out_ref, sems = refs
    count, tok, ch = upd_ref.shape
    cols = tok // rows
    if fresh:
        for a in range(3):
            for b in range(3):
                wide_ref[a * ch:(a + 1) * ch, b * ch:(b + 1) * ch] = w_ref[a, b]
    else:
        wide_ref = w_ref

    stats = jnp.concatenate([stat_ref[i] + top_ref[i, cols:cols + 8] if pair else stat_ref[i]
                             for i in range(count)], axis=0)
    width = ch // GROUPS
    first = lax.broadcasted_iota(I32, (ch, ch), 0)
    second = lax.broadcasted_iota(I32, (ch, ch), 1)
    group_of = lambda v: (v * (65536 // width + 1)) >> 16
    same = jnp.where(group_of(first) == group_of(second), 1.0, 0.0).astype(BF16)
    high = stats.astype(BF16)
    rest = stats - high.astype(F32)
    middle = rest.astype(BF16)
    low = (rest - middle.astype(F32)).astype(BF16)
    grouped = (dot(high, same) + dot(middle, same) + dot(low, same)) / counted
    gain = gn_ref[...].astype(F32).reshape(1, ch)
    bias = bias_ref[...].astype(F32).reshape(1, ch)
    me = lax.axis_index("row")
    column = lax.broadcasted_iota(I32, (tok, ch), 0) % cols
    copies = []
    for i in range(count):
        mean = grouped[8 * i:8 * i + 1]
        scale = lax.rsqrt(grouped[8 * i + 1:8 * i + 2] - mean * mean + 1e-05) * gain

        def activated(u):
            v = (u.astype(F32) - mean) * scale
            return (v / (1.0 + jnp.exp(-v))).astype(BF16)

        above = jnp.where(me > 0, activated(top_ref[i, 0:cols]), jnp.zeros((cols, ch), BF16))
        below = jnp.where(me < lax.axis_size("row") - 1, activated(bot_ref[i, 0:cols]), jnp.zeros((cols, ch), BF16))
        inner = activated(upd_ref[i])
        act_ref[:, ch:2 * ch] = inner
        act_ref[0:cols, 0:ch] = above
        act_ref[cols:tok, 0:ch] = inner[0:tok - cols]
        act_ref[0:tok - cols, 2 * ch:] = inner[cols:tok]
        act_ref[tok - cols:tok, 2 * ch:] = below
        parts = dot(act_ref[...], wide_ref[...])
        left = jnp.where(column == 0, 0.0, pltpu.roll(parts[:, 0:ch], 1, 0))
        right = jnp.where(column == cols - 1, 0.0, pltpu.roll(parts[:, 2 * ch:], tok - 1, 0))
        out_ref[i] = (upd_ref[i].astype(F32) + (left + parts[:, ch:2 * ch] + right) + bias).astype(BF16)
        copies.append(pltpu.make_async_copy(out_ref.at[i], out_hbm.at[start + i], sems.at[i]))
        copies[-1].start()
    for copy in copies:
        copy.wait()


def conv(start, frames, upd, top, bot, stats, gn, bias, weight, rows, pair, counted, into=None):
    count, tok, ch = upd.shape
    fresh = into is None
    args = [upd, top, bot, stats, gn, bias, weight if fresh else into[1]]
    outs = [far_of(frames, tok, ch)] + ([near_of(3 * ch, 3 * ch)] if fresh else [])
    scratch = [pltpu.VMEM((tok, 3 * ch), BF16), pltpu.VMEM((count, tok, ch), BF16),
               pltpu.SemaphoreType.DMA((count,))]
    got = kernel_call(functools.partial(conv_kernel, start, rows, counted, pair, fresh), "conv",
                      args, [] if fresh else [into[0]], outs, scratch, cost(count * tok * ch * ch * 30, 4e6),
                      {} if fresh else {len(args): 0})
    return got[0], got[1] if fresh else into[1]


def fan(value, axis, heads, steps):
    size = lax.axis_size(axis)
    got = {}
    for k in steps:
        route = [(i, i + k) for i in heads if i + k < size]
        if route:
            got[k] = lax.ppermute(value, axis, route)
    return got


def chosen(value, axis, got, modulus):
    place = lax.axis_index(axis) % modulus
    for k, arrived in got.items():
        value = jnp.where(place == k, arrived, value)
    return value


def others(value, rows):
    got = [lax.ppermute(value, "row", [(i, (i + k) % rows) for i in range(rows)]) for k in range(1, rows)]
    return got[0] if len(got) == 1 else jnp.concatenate(got, axis=2)


def body(latents, ln_gain, q_weight, k_weight, v_weight, o_weight, gn_gain, conv_weight, conv_bias):
    frames, row_count, cols, ch = latents.shape
    tok = row_count * cols
    size, blocks = lax.axis_size("row"), lax.axis_size("frame")
    pair = size == 2
    x = latents.reshape(frames, tok, ch)

    qt, main, lead, tail, wkp, wvt, wop = project(x, ln_gain, q_weight, k_weight, v_weight, o_weight)
    common = (qt, wkp, wvt)
    routes = [[(f * size + r, (f + 1) * size + (r + k) % size) for f in range(blocks - 1) for r in range(size)]
              for k in range(size)]
    inner = 1
    while inner * inner < blocks:
        inner *= 2
    side = others(main, size)
    prev = lax.ppermute(tail, ("frame", "row"), routes[0])
    spread = fan(lead, "frame", [0], range(inner, blocks, inner))
    state = flash(own_kernel, "own", *common, [main], None, frames - 1)

    state, spread = lax.optimization_barrier((state, spread))
    side, tail = lax.optimization_barrier((side, tail))
    came = [lax.ppermute(tail, ("frame", "row"), route) for route in routes[1:]]
    prev_side = came[0] if pair else jnp.concatenate(came, axis=2)
    lead = chosen(lead, "frame", spread, blocks)
    spread = fan(lead, "frame", range(0, blocks, inner), range(1, inner))
    state = flash(side_kernel, "side", *common, [prev, main, side], state, frames)

    state, spread = lax.optimization_barrier((state, spread))
    lead = chosen(lead, "frame", spread, inner)
    lead_side = others(lead, size)
    state = flash(lead_kernel, "lead", *common, [prev_side, side, lead], state, frames + 1)

    half = frames // 2
    made, into, finished = None, None, []
    for start, count in ((0, half), (half, frames - half)):
        (upd, edge, stats), made = finish(start, count, *common, wop, state, lead_side, made, x, row_count, pair)
        if pair:
            top = bot = lax.ppermute(edge, "row", [(0, 1), (1, 0)])
        else:
            top = lax.ppermute(edge[:, cols:], "row", [(i, i + 1) for i in range(size - 1)])
            bot = lax.ppermute(edge[:, :cols], "row", [(i + 1, i) for i in range(size - 1)])
            stats = lax.psum(stats, "row")
        finished.append((start, upd, top, bot, stats))
    for start, upd, top, bot, stats in finished:
        into = conv(start, frames, upd, top, bot, stats, gn_gain, conv_bias, conv_weight,
                    row_count, pair, tok * size * (ch // GROUPS), into)
    return into[0].reshape(latents.shape)


def solution(mesh):
    in_specs = (P("frame", "row", None, None), P(), P(), P(), P(), P(), P(), P(), P())
    out_specs = P("frame", "row", None, None)
    return jax.shard_map(body, mesh=mesh, in_specs=in_specs, out_specs=out_specs, check_vma=False)
```

time: 487 us -> 94.6 us (0.19); the launches traced: 480 us -> 94.1 us
  matrix products: 139 us -> 0 us
  waiting for transfers between devices: 117 us -> 0.29 us
  local copies, waits for them, and re-layouts: 108 us -> 0.01 us
  other arithmetic: 76 us -> 2.87 us
  Pallas kernels: 0 us -> 65.9 us
  between operations: 14.2 us -> 0.38 us
  blocking collectives: 4.93 us -> 0 us
    dot_general x20 -> x0, matrix products: 139 us -> none  [the longest x4 66.9 us: single(): jnp.einsum('qhd,khd->hqk', frame_queries, all_keys, preferred_element_typ...]
    psum x1 -> x0, waiting for transfers between devices: 73.9 us -> none  [spread_2(): return lax.psum(kept, axis)]
    pallas_call x0 -> x8, Pallas kernels: none -> 65.9 us  [kernel_call(): pl.pallas_call(body, in_specs=[in_vmem] * len(near_args) + [anywhere] * l...]
    reduce_sum x7 -> x0, other arithmetic: 61.8 us -> none  [the longest x4 56.1 us: single(): totals = jnp.sum(raised, axis=-1)]
    all_to_all x3 -> x0, waiting for transfers between devices: 43.4 us -> none  [the longest x1 29.6 us: body(): lax.all_to_all(sent_pairs, 'row', split_axis=3, concat_axis=1, tiled=True)]
    unnamed x35 -> x6, local copies, waits for them, and re-layouts: 23.3 us -> 0.01 us
    all_to_all x4 -> x0, local copies, waits for them, and re-layouts: 22.8 us -> none  [the longest x2 12.4 us: body(): lax.all_to_all(sent_pairs, 'row', split_axis=3, concat_axis=1, tiled=True)]
    ppermute x3 -> x12, starting transfers between devices: 6.96 us -> 24.7 us  [the longest x6 16.4 us: fan(): got[k] = lax.ppermute(value, axis, route)]
  transfers between devices with their start and end apart: 7 -> 12, of which waited for: 3 -> 1; matrix products, arithmetic and copies ran while one was open for 10% -> 3% of each run, Pallas kernels for 0% -> 53%
where the time goes in v3:
time: 94.6 us; the launch traced here: 94.1 us
  Pallas kernels  65.9 us (70%)
  starting transfers between devices  24.7 us (26%)
  other arithmetic  2.87 us (3%)
    pallas_call x8, Pallas kernels, kernel_call(): pl.pallas_call(body, in_specs=[in_vmem] * len(near_args) + [anywhere] * l...  65.9 us
    ppermute x6, starting transfers between devices, fan(): got[k] = lax.ppermute(value, axis, route)  16.4 us
    ppermute x2, starting transfers between devices, others(): lax.ppermute(value, 'row', [(i, (i + k) % rows) for i in range(rows)])  3.61 us
    select_n x2, other arithmetic, chosen(): value = jnp.where(place == k, arrived, value)  2.87 us
    ppermute x2, starting transfers between devices, body(): top = bot = lax.ppermute(edge, 'row', [(0, 1), (1, 0)])  2.14 us
  transfers between devices with their start and end apart: 12, of which 1 were waited for; matrix products, arithmetic and copies ran while one was open for 3% of the time, Pallas kernels for 53%

profile of v3, /device:TPU:0, one launch (start us, length us, event | category | flops | bytes accessed | tf_op | source)
XLA Modules:
  0.0 94.1 jit_solution(13047086870465444161)
XLA Ops:
  0.0 5.6 %project.1 = (bf16[4,512,512]{2,1,0:T(8,128)(2,1)S(1)}, bf16[3,320,512]{2,1,0:T(8,128)(2,1)}, bf16[1,320,512]{2,1,0:T(8,128)(2,1)}, bf16[1,320,512]{2,1,0:T(8,12...) custom-call(bf16[4,512,320]{2,1,0:T(8,128)(2,1)} %bitcast.2, ...), custom_call_target="tpu_custom_call" | custom-call | flops 335544320 | bytes 800000 | tf_op jit(solution)/shard_map/project/pallas_call | solution.py:54
  5.6 3.0 %collective-permute-start.1 = (bf16[3,320,512]{2,1,0:T(8,128)(2,1)}, bf16[3,320,512]{2,1,0:T(8,128)(2,1)}, u32[]{:S(2)}, u32[]{:S(2)}) collective-permute-start(bf16[3,320,512]{2,1,0:T(8,128)(2,1)} %get-tuple-element.37.main_ref), channel_id=1, source_target_pairs={{0,1},{1,0},{2,3},{3,2},{4,5},{5,4},{6,7},{7,6},{8,9},{9,8},{10,11... | collective-permute-start | bytes 2949128 | tf_op jit(solution)/shard_map/ppermute | solution.py:443
  8.6 6.2 %collective-permute-start.4 = (bf16[1,320,512]{2,1,0:T(8,128)(2,1)}, bf16[1,320,512]{2,1,0:T(8,128)(2,1)}, u32[]{:S(2)}, u32[]{:S(2)}) collective-permute-start(bf16[1,320,512]{2,1,0:T(8,128)(2,1)} %get-tuple-element.39), channel_id=1, source_target_pairs={{0,24},{1,25}} | collective-permute-start | bytes 983048 | tf_op jit(solution)/shard_map/ppermute | solution.py:431
  14.9 2.0 %collective-permute-start.3 = (bf16[1,320,512]{2,1,0:T(8,128)(2,1)}, bf16[1,320,512]{2,1,0:T(8,128)(2,1)}, u32[]{:S(2)}, u32[]{:S(2)}) collective-permute-start(bf16[1,320,512]{2,1,0:T(8,128)(2,1)} %get-tuple-element.39), channel_id=1, source_target_pairs={{0,16},{1,17}} | collective-permute-start | bytes 983048 | tf_op jit(solution)/shard_map/ppermute | solution.py:431
  16.9 2.0 %collective-permute-start.2 = (bf16[1,320,512]{2,1,0:T(8,128)(2,1)}, bf16[1,320,512]{2,1,0:T(8,128)(2,1)}, u32[]{:S(2)}, u32[]{:S(2)}) collective-permute-start(bf16[1,320,512]{2,1,0:T(8,128)(2,1)} %get-tuple-element.39), channel_id=1, source_target_pairs={{0,8},{1,9}} | collective-permute-start | bytes 983048 | tf_op jit(solution)/shard_map/ppermute | solution.py:431
  18.9 1.3 %collective-permute-start = (bf16[1,320,512]{2,1,0:T(8,128)(2,1)}, bf16[1,320,512]{2,1,0:T(8,128)(2,1)S(1)}, u32[]{:S(2)}, u32[]{:S(2)}) collective-permute-start(bf16[1,320,512]{2,1,0:T(8,128)(2,1)} %get-tuple-element.47), channel_id=1, source_target_pairs={{0,2},{1,3},{2,4},{3,5},{4,6},{5,7},{6,8},{7,9},{8,10},{9,11},{10,... | collective-permute-start | bytes 983048 | tf_op jit(solution)/shard_map/ppermute | solution.py:462
  20.2 10.4 %own.1.state_in = f32[4,384,512]{2,1,0:T(8,128)} custom-call(bf16[4,512,512]{2,1,0:T(8,128)(2,1)S(1)} %get-tuple-element.32.qt_ref.refs_0_, bf16[320,512]{1,0:T(8,128)(2,1)S(1)} %get-tuple-element.33.wkp_ref.refs_1_, bf16[384,320]{1,0:T(8,128)(2,1)S(1)} %get-tuple-element.34.wvt_ref.refs_2_, bf16[3,320,512]{2,1,0:T(8,128)(2,1)} %get-tuple-element.37.main_ref), custom_call_target="tpu_custom_call" | custom-call | flops 880803840 | bytes 78643 | tf_op jit(solution)/shard_map/own/pallas_call | solution.py:54
  30.6 0.0 collective-permute-done.4
  30.7 0.0 collective-permute-done.3
  30.7 0.0 collective-permute-done.2
  30.7 1.8 %select_select_fusion.1 = bf16[1,320,512]{2,1,0:T(8,128)(2,1)} fusion(bf16[1,320,512]{2,1,0:T(8,128)(2,1)} %collective-permute-done.4, bf16[1,320,512]{2,1,0:T(8,128)(2,1)} %collective-permute-done.3, bf16[1,320,512]{2,1,0:T(8,128)(2,1)} %collective-permute-done.2, bf16[1,320,512]{2,1,0:T(8,128)(2,1)} %get-tuple-element.39, pred[]{:T(512)S(6)} %eq.24, ...), kind=kLoop, calls=%fused_computation.1 | loop fusion | flops 491520 | bytes 1638403 | tf_op jit(solution)/shard_map/jit(_where)/select_n | solution.py:438
  32.5 2.0 %collective-permute-start.7 = (bf16[1,320,512]{2,1,0:T(8,128)(2,1)}, bf16[1,320,512]{2,1,0:T(8,128)(2,1)}, u32[]{:S(2)}, u32[]{:S(2)}) collective-permute-start(bf16[1,320,512]{2,1,0:T(8,128)(2,1)} %select_select_fusion.1), channel_id=1, source_target_pairs={{0,6},{8,14},{16,22},{24,30},{1,7},{9,15},{17,23},{25,31}} | collective-permute-start | bytes 983048 | tf_op jit(solution)/shard_map/ppermute | solution.py:431
  34.5 2.0 %collective-permute-start.6 = (bf16[1,320,512]{2,1,0:T(8,128)(2,1)}, bf16[1,320,512]{2,1,0:T(8,128)(2,1)}, u32[]{:S(2)}, u32[]{:S(2)}) collective-permute-start(bf16[1,320,512]{2,1,0:T(8,128)(2,1)} %select_select_fusion.1), channel_id=1, source_target_pairs={{0,4},{8,12},{16,20},{24,28},{1,5},{9,13},{17,21},{25,29}} | collective-permute-start | bytes 983048 | tf_op jit(solution)/shard_map/ppermute | solution.py:431
  36.5 2.0 %collective-permute-start.5 = (bf16[1,320,512]{2,1,0:T(8,128)(2,1)}, bf16[1,320,512]{2,1,0:T(8,128)(2,1)}, u32[]{:S(2)}, u32[]{:S(2)}) collective-permute-start(bf16[1,320,512]{2,1,0:T(8,128)(2,1)} %select_select_fusion.1), channel_id=1, source_target_pairs={{0,2},{8,10},{16,18},{24,26},{1,3},{9,11},{17,19},{25,27}} | collective-permute-start | bytes 983048 | tf_op jit(solution)/shard_map/ppermute | solution.py:431
  38.6 0.0 collective-permute-done.1.side_ref
  38.6 1.3 %collective-permute-start.9 = (bf16[1,320,512]{2,1,0:T(8,128)(2,1)}, bf16[1,320,512]{2,1,0:T(8,128)(2,1)S(1)}, u32[]{:S(2)}, u32[]{:S(2)}) collective-permute-start(bf16[1,320,512]{2,1,0:T(8,128)(2,1)} %get-tuple-element.47), channel_id=1, source_target_pairs={{0,3},{1,2},{2,5},{3,4},{4,7},{5,6},{6,9},{7,8},{8,11},{9,10},{10,... | collective-permute-start | bytes 983048 | tf_op jit(solution)/shard_map/ppermute | solution.py:468
  39.9 0.0 collective-permute-done.prev_ref
  39.9 13.4 %side.1.state_in = f32[4,384,512]{2,1,0:T(8,128)} custom-call(bf16[4,512,512]{2,1,0:T(8,128)(2,1)S(1)} %get-tuple-element.32.qt_ref.refs_0_, bf16[320,512]{1,0:T(8,128)(2,1)S(1)} %get-tuple-element.33.wkp_ref.refs_1_, bf16[384,320]{1,0:T(8,128)(2,1)S(1)} %get-tuple-element.34.wvt_ref.refs_2_, ...), custom_call_target="tpu_custom_call", output_to_operand_aliasing={{}: (6, {})} | custom-call | flops 1174405120 | bytes 104857 | tf_op jit(solution)/shard_map/side/pallas_call | solution.py:54
  53.3 0.0 collective-permute-done.7
  53.3 0.0 collective-permute-done.6
  53.4 0.0 collective-permute-done.5
  53.4 1.1 %select_select_fusion.lead_ref = bf16[1,320,512]{2,1,0:T(8,128)(2,1)S(1)} fusion(bf16[1,320,512]{2,1,0:T(8,128)(2,1)} %collective-permute-done.7, bf16[1,320,512]{2,1,0:T(8,128)(2,1)} %collective-permute-done.6, bf16[1,320,512]{2,1,0:T(8,128)(2,1)} %collective-permute-done.5, bf16[1,320,512]{2,1,0:T(8,128)(2,1)} %select_select_fusion.1, pred[]{:T(512)S(6)} %eq.26, ...), kind=kLoop, calls=%fused_computation | loop fusion | flops 491520 | bytes 1638403 | tf_op jit(solution)/shard_map/jit(_where)/select_n | solution.py:438
  54.4 0.6 collective-permute-start.8
  55.0 0.0 collective-permute-done.9.prev_ref
  55.0 14.5 %lead.1.refs_5_.refs_6_ = f32[4,384,512]{2,1,0:T(8,128)} custom-call(bf16[4,512,512]{2,1,0:T(8,128)(2,1)S(1)} %get-tuple-element.32.qt_ref.refs_0_, bf16[320,512]{1,0:T(8,128)(2,1)S(1)} %get-tuple-element.33.wkp_ref.refs_1_, bf16[384,320]{1,0:T(8,128)(2,1)S(1)} %get-tuple-element.34.wvt_ref.refs_2_, ...), custom_call_target="tpu_custom_call", output_to_operand_aliasing={{}: (6, {})} | custom-call | flops 1468006400 | bytes 131072 | tf_op jit(solution)/shard_map/lead/pallas_call | solution.py:54
  69.5 0.0 collective-permute-done.8.refs_4_
  69.5 6.7 %finish.2 = (bf16[2,512,320]{2,1,0:T(8,128)(2,1)S(1)}, f32[2,40,320]{2,1,0:T(8,128)S(1)}, f32[2,8,320]{2,1,0:T(8,128)S(1)}, bf16[512,512]{1,0:T(8,128)(2,1)S(1)}, bf16[384,512]{1,0:T(8,128)(2,1)S(1)}) custom-call(bf16[4,512,512]{2,1,0:T(8,128)(2,1)S(1)} %get-tuple-element.32.qt_ref.refs_0_, bf16[320,512]{1,0:T(8,128)(2,1)S(1)} %get-tuple-element.33.wkp_ref.refs_1_, ...), custom_call_target="tpu_custom_call" | custom-call | flops 587202560 | bytes 52428 | tf_op jit(solution)/shard_map/finish/pallas_call | solution.py:54
  76.2 1.6 %collective-permute-start.11 = (f32[2,40,320]{2,1,0:T(8,128)S(1)}, f32[2,40,320]{2,1,0:T(8,128)S(1)}, u32[]{:S(2)}, u32[]{:S(2)}) collective-permute-start(f32[2,40,320]{2,1,0:T(8,128)S(1)} %get-tuple-element.55), channel_id=1, source_target_pairs={{0,1},{1,0},{2,3},{3,2},{4,5},{5,4},{6,7},{7,6},{8,9},{9,8},{10,11... | collective-permute-start | bytes 307208 | tf_op jit(solution)/shard_map/ppermute | solution.py:484
  77.8 0.0 copy-start
  77.8 0.0 copy-start.1
  77.8 0.0 copy-start.2
  77.8 7.1 %finish.3 = (bf16[2,512,320]{2,1,0:T(8,128)(2,1)S(1)}, f32[2,40,320]{2,1,0:T(8,128)S(1)}, f32[2,8,320]{2,1,0:T(8,128)S(1)}) custom-call(bf16[4,512,512]{2,1,0:T(8,128)(2,1)S(1)} %get-tuple-element.32.qt_ref.refs_0_, bf16[320,512]{1,0:T(8,128)(2,1)S(1)} %get-tuple-element.33.wkp_ref.refs_1_, bf16[384,320]{1,0:T(8,128)(2,1)S(1)} %get-tuple-element.34.wvt_ref.refs_2_, ...), custom_call_target="tpu_custom_call" | custom-call | flops 587202560 | bytes 52428 | tf_op jit(solution)/shard_map/finish/pallas_call | solution.py:54
  84.9 0.6 collective-permute-start.10
  85.5 0.0 collective-permute-done.11.refs_1_.refs_2_
  85.5 0.0 copy-done
  85.5 0.0 copy-done.1
  85.5 0.0 copy-done.2
  85.5 4.1 %conv.2 = (bf16[4,512,320]{2,1,0:T(8,128)(2,1)}, bf16[960,960]{1,0:T(8,128)(2,1)S(1)}) custom-call(bf16[2,512,320]{2,1,0:T(8,128)(2,1)S(1)} %get-tuple-element.54.refs_0_, f32[2,40,320]{2,1,0:T(8,128)S(1)} %collective-permute-done.11.refs_1_.refs_2_, f32[2,40,320]{2,1,0:T(8,128)S(1)} %collective-permute-done.11.refs_1_.refs_2_, ...), custom_call_target="tpu_custom_call" | custom-call | flops 3145728000 | bytes 4000000 | tf_op jit(solution)/shard_map/conv/pallas_call | solution.py:54
  89.6 0.3 collective-permute-done.10.refs_1_.refs_2_
  89.9 4.0 %conv.3 = bf16[4,512,320]{2,1,0:T(8,128)(2,1)} custom-call(bf16[2,512,320]{2,1,0:T(8,128)(2,1)S(1)} %get-tuple-element.51.refs_0_, f32[2,40,320]{2,1,0:T(8,128)S(1)} %collective-permute-done.10.refs_1_.refs_2_, f32[2,40,320]{2,1,0:T(8,128)S(1)} %collective-permute-done.10.refs_1_.refs_2_, ...), custom_call_target="tpu_custom_call", output_to_operand_aliasing={{}: (7, {})} | custom-call | flops 3145728000 | bytes 4000000 | tf_op jit(solution)/shard_map/conv/pallas_call | solution.py:54
Async XLA Ops:
  5.6 33.0 %collective-permute-start.1 = (bf16[3,320,512]{2,1,0:T(8,128)(2,1)}, bf16[3,320,512]{2,1,0:T(8,128)(2,1)}, u32[]{:S(2)}, u32[]{:S(2)}) collective-permute-start(bf16[3,320,512]{2,1,0:T(8,128)(2,1)} %get-tuple-element.37.main_ref), channel_id=1, source_target_pairs={{0,1},{1,0},{2,3},{3,2},{4,5},{5,4},{6,7},{7,6},{8,9},{9,8},{10,11... | collective-permute-start | bytes 2949128 | tf_op jit(solution)/shard_map/ppermute | solution.py:443
  8.6 22.0 %collective-permute-start.4 = (bf16[1,320,512]{2,1,0:T(8,128)(2,1)}, bf16[1,320,512]{2,1,0:T(8,128)(2,1)}, u32[]{:S(2)}, u32[]{:S(2)}) collective-permute-start(bf16[1,320,512]{2,1,0:T(8,128)(2,1)} %get-tuple-element.39), channel_id=1, source_target_pairs={{0,24},{1,25}} | collective-permute-start | bytes 983048 | tf_op jit(solution)/shard_map/ppermute | solution.py:431
  14.9 15.8 %collective-permute-start.3 = (bf16[1,320,512]{2,1,0:T(8,128)(2,1)}, bf16[1,320,512]{2,1,0:T(8,128)(2,1)}, u32[]{:S(2)}, u32[]{:S(2)}) collective-permute-start(bf16[1,320,512]{2,1,0:T(8,128)(2,1)} %get-tuple-element.39), channel_id=1, source_target_pairs={{0,16},{1,17}} | collective-permute-start | bytes 983048 | tf_op jit(solution)/shard_map/ppermute | solution.py:431
  16.9 13.8 %collective-permute-start.2 = (bf16[1,320,512]{2,1,0:T(8,128)(2,1)}, bf16[1,320,512]{2,1,0:T(8,128)(2,1)}, u32[]{:S(2)}, u32[]{:S(2)}) collective-permute-start(bf16[1,320,512]{2,1,0:T(8,128)(2,1)} %get-tuple-element.39), channel_id=1, source_target_pairs={{0,8},{1,9}} | collective-permute-start | bytes 983048 | tf_op jit(solution)/shard_map/ppermute | solution.py:431
  18.9 20.9 %collective-permute-start = (bf16[1,320,512]{2,1,0:T(8,128)(2,1)}, bf16[1,320,512]{2,1,0:T(8,128)(2,1)S(1)}, u32[]{:S(2)}, u32[]{:S(2)}) collective-permute-start(bf16[1,320,512]{2,1,0:T(8,128)(2,1)} %get-tuple-element.47), channel_id=1, source_target_pairs={{0,2},{1,3},{2,4},{3,5},{4,6},{5,7},{6,8},{7,9},{8,10},{9,11},{10,... | collective-permute-start | bytes 983048 | tf_op jit(solution)/shard_map/ppermute | solution.py:462
  32.5 20.9 %collective-permute-start.7 = (bf16[1,320,512]{2,1,0:T(8,128)(2,1)}, bf16[1,320,512]{2,1,0:T(8,128)(2,1)}, u32[]{:S(2)}, u32[]{:S(2)}) collective-permute-start(bf16[1,320,512]{2,1,0:T(8,128)(2,1)} %select_select_fusion.1), channel_id=1, source_target_pairs={{0,6},{8,14},{16,22},{24,30},{1,7},{9,15},{17,23},{25,31}} | collective-permute-start | bytes 983048 | tf_op jit(solution)/shard_map/ppermute | solution.py:431
  34.5 18.8 %collective-permute-start.6 = (bf16[1,320,512]{2,1,0:T(8,128)(2,1)}, bf16[1,320,512]{2,1,0:T(8,128)(2,1)}, u32[]{:S(2)}, u32[]{:S(2)}) collective-permute-start(bf16[1,320,512]{2,1,0:T(8,128)(2,1)} %select_select_fusion.1), channel_id=1, source_target_pairs={{0,4},{8,12},{16,20},{24,28},{1,5},{9,13},{17,21},{25,29}} | collective-permute-start | bytes 983048 | tf_op jit(solution)/shard_map/ppermute | solution.py:431
  36.5 16.8 %collective-permute-start.5 = (bf16[1,320,512]{2,1,0:T(8,128)(2,1)}, bf16[1,320,512]{2,1,0:T(8,128)(2,1)}, u32[]{:S(2)}, u32[]{:S(2)}) collective-permute-start(bf16[1,320,512]{2,1,0:T(8,128)(2,1)} %select_select_fusion.1), channel_id=1, source_target_pairs={{0,2},{8,10},{16,18},{24,26},{1,3},{9,11},{17,19},{25,27}} | collective-permute-start | bytes 983048 | tf_op jit(solution)/shard_map/ppermute | solution.py:431
  38.6 16.5 %collective-permute-start.9 = (bf16[1,320,512]{2,1,0:T(8,128)(2,1)}, bf16[1,320,512]{2,1,0:T(8,128)(2,1)S(1)}, u32[]{:S(2)}, u32[]{:S(2)}) collective-permute-start(bf16[1,320,512]{2,1,0:T(8,128)(2,1)} %get-tuple-element.47), channel_id=1, source_target_pairs={{0,3},{1,2},{2,5},{3,4},{4,7},{5,6},{6,9},{7,8},{8,11},{9,10},{10,... | collective-permute-start | bytes 983048 | tf_op jit(solution)/shard_map/ppermute | solution.py:468
  54.4 15.1 %collective-permute-start.8 = (bf16[1,320,512]{2,1,0:T(8,128)(2,1)S(1)}, bf16[1,320,512]{2,1,0:T(8,128)(2,1)S(1)}, u32[]{:S(2)}, u32[]{:S(2)}) collective-permute-start(bf16[1,320,512]{2,1,0:T(8,128)(2,1)S(1)} %select_select_fusion.lead_ref), channel_id=1, source_target_pairs={{0,1},{1,0},{2,3},{3,2},{4,5},{5,4},{6,7},{7,6},{8,9},{9,8},{10,11... | collective-permute-start | bytes 983048 | tf_op jit(solution)/shard_map/ppermute | solution.py:443
  76.2 9.3 %collective-permute-start.11 = (f32[2,40,320]{2,1,0:T(8,128)S(1)}, f32[2,40,320]{2,1,0:T(8,128)S(1)}, u32[]{:S(2)}, u32[]{:S(2)}) collective-permute-start(f32[2,40,320]{2,1,0:T(8,128)S(1)} %get-tuple-element.55), channel_id=1, source_target_pairs={{0,1},{1,0},{2,3},{3,2},{4,5},{5,4},{6,7},{7,6},{8,9},{9,8},{10,11... | collective-permute-start | bytes 307208 | tf_op jit(solution)/shard_map/ppermute | solution.py:484
  77.8 7.7 %copy-start = (bf16[3,3,320,320]{3,2,1,0:T(8,128)(2,1)S(1)}, bf16[3,3,320,320]{3,2,1,0:T(8,128)(2,1)}, u32[]{:S(2)}) copy-start(bf16[3,3,320,320]{3,2,1,0:T(8,128)(2,1)} %refs_6_.1) | copy-start | bytes 5529604
  77.8 7.7 %copy-start.1 = (bf16[320]{0:T(512)(128)(2,1)S(1)}, bf16[320]{0:T(512)(128)(2,1)}, u32[]{:S(2)}) copy-start(bf16[320]{0:T(512)(128)(2,1)} %refs_4_.3) | copy-start | bytes 1924
  77.8 7.7 %copy-start.2 = (bf16[320]{0:T(512)(128)(2,1)S(1)}, bf16[320]{0:T(512)(128)(2,1)}, u32[]{:S(2)}) copy-start(bf16[320]{0:T(512)(128)(2,1)} %refs_5_.3) | copy-start | bytes 1924
  84.9 4.9 %collective-permute-start.10 = (f32[2,40,320]{2,1,0:T(8,128)S(1)}, f32[2,40,320]{2,1,0:T(8,128)S(1)}, u32[]{:S(2)}, u32[]{:S(2)}) collective-permute-start(f32[2,40,320]{2,1,0:T(8,128)S(1)} %get-tuple-element.52), channel_id=1, source_target_pairs={{0,1},{1,0},{2,3},{3,2},{4,5},{5,4},{6,7},{7,6},{8,9},{9,8},{10,11... | collective-permute-start | bytes 307208 | tf_op jit(solution)/shard_map/ppermute | solution.py:484
